TPU v7x, 32 devices: a whole 2x2x4 slice. The times are simulated.
32 devices in a mesh: mem: 4 (over z), dp: 8 (over y, x, core).
Axes of the slice: x: 2, y: 2, z: 4, core: 2. Of those that a mesh axis runs over, the one named last changes fastest.
Arguments:
- block_input: bfloat16 [8, 4, 256, 1024], P('dp', 'mem'), may hold values from -6 to 6
- memory: bfloat16 [8, 4, 512, 1024], P('dp', None, 'mem'), may hold values from -6 to 6
- out_grad: bfloat16 [8, 4, 256, 1024], P('dp', 'mem'), may hold values from -6 to 6
- decoder_segments: int32 [8, 4, 256], P('dp', 'mem'), may hold values from 0 to 7, as said below
- encoder_segments: int32 [8, 4, 512], P('dp', 'mem'), may hold values from 0 to 7, as said below
- distance_buckets: int32 [256], replicated, may hold values from 0 to 31, as said below
- self_gain: float32 [1024], replicated, may hold values from 0.1 to 1.9
- cross_gain: float32 [1024], replicated, may hold values from 0.1 to 1.9
- ffn_gain: float32 [1024], replicated, may hold values from 0.1 to 1.9
- position_bias: float32 [32, 16], replicated, may hold values from -4 to 4
- self_query: bfloat16 [1024, 1024], P(('mem', 'dp')), may hold values from -0.1875 to 0.1875
- self_key: bfloat16 [1024, 512], P(('mem', 'dp')), may hold values from -0.1875 to 0.1875
- self_value: bfloat16 [1024, 512], P(('mem', 'dp')), may hold values from -0.1875 to 0.1875
- self_out: bfloat16 [1024, 1024], P(('mem', 'dp')), may hold values from -0.75 to 0.75
- cross_query: bfloat16 [1024, 1024], P(('mem', 'dp')), may hold values from -0.1875 to 0.1875
- cross_key: bfloat16 [1024, 512], P(('mem', 'dp')), may hold values from -0.1875 to 0.1875
- cross_value: bfloat16 [1024, 512], P(('mem', 'dp')), may hold values from -0.1875 to 0.1875
- cross_out: bfloat16 [1024, 1024], P(('mem', 'dp')), may hold values from -1 to 1
- ffn_gate: bfloat16 [1024, 2816], P(('mem', 'dp')), may hold values from -0.1875 to 0.1875
- ffn_up: bfloat16 [1024, 2816], P(('mem', 'dp')), may hold values from -0.1875 to 0.1875
- ffn_down: bfloat16 [1024, 2816], P(('mem', 'dp')), may hold values from -0.15625 to 0.15625
Outputs:
- result: bfloat16 [8, 4, 256, 1024], P('dp', 'mem')
- input_grad: float32 [8, 4, 256, 1024], P('dp', 'mem')
- memory_grad: float32 [8, 4, 512, 1024], P('dp', None, 'mem')
- self_gain_grad: float32 [1024], replicated
- cross_gain_grad: float32 [1024], replicated
- ffn_gain_grad: float32 [1024], replicated
- position_bias_grad: float32 [32, 16], replicated
- self_query_grad: float32 [1024, 1024], P(('mem', 'dp'))
- self_key_grad: float32 [1024, 512], P(('mem', 'dp'))
- self_value_grad: float32 [1024, 512], P(('mem', 'dp'))
- self_out_grad: float32 [1024, 1024], P(('mem', 'dp'))
- cross_query_grad: float32 [1024, 1024], P(('mem', 'dp'))
- cross_key_grad: float32 [1024, 512], P(('mem', 'dp'))
- cross_value_grad: float32 [1024, 512], P(('mem', 'dp'))
- cross_out_grad: float32 [1024, 1024], P(('mem', 'dp'))
- ffn_gate_grad: float32 [1024, 2816], P(('mem', 'dp'))
- ffn_up_grad: float32 [1024, 2816], P(('mem', 'dp'))
- ffn_down_grad: float32 [1024, 2816], P(('mem', 'dp'))
Inputs may be any that keep to these rules, and one draw needn't show every extreme that they name: `decoder_segments`: within each row the ids never fall, and every document 0 to 7 has one or more tokens. `encoder_segments`: every aligned run of 8 positions of a row holds each document once. `distance_buckets`: never falls as the distance grows; distance 0 has bucket 0 and every bucket occurs.
All inputs are finite; a program needn't handle non-finite values.
Results may differ from a plain program's by a relative error of at most 0.018.
Values may be sent and summed in bfloat16 or wider, within the bound.
No kernel may reach another device: no remote copies, remote signals or barrier semaphores. Data moves between devices by JAX's collectives and lax.ppermute only.
A program may use at most 256 MiB of HBM per device.

v0:
```python
import math

import jax
import jax.numpy as jnp
from jax import lax
from jax.sharding import PartitionSpec as P

DH = 64


EPSILON = 1e-06
NEGATIVE = -1e30
HIGHEST = lax.Precision.HIGHEST


def norm_rows(stream, gain):
    scale = lax.rsqrt(jnp.mean(stream * stream, axis=-1, keepdims=True) + EPSILON)
    return (stream * scale * gain, scale)


def norm_back(stream, scale, gain, normed_grad):
    weighted = normed_grad * gain
    inner = jnp.mean(weighted * stream, axis=-1, keepdims=True)
    stream_grad = scale * weighted - stream * (scale * scale * scale) * inner
    gain_grad = jnp.sum((normed_grad * stream * scale).reshape(-1, stream.shape[-1]), axis=0)
    return (stream_grad, gain_grad)


def project(left, weight):
    return jnp.einsum("...d,dc->...c", left, weight, preferred_element_type=jnp.float32)


def project_back(left, weight):
    return jnp.einsum("...c,dc->...d", left, weight, preferred_element_type=jnp.float32)


def weight_grad(left, right):
    flat_left = left.reshape(-1, left.shape[-1])
    flat_right = right.reshape(-1, right.shape[-1])
    return lax.dot_general(
        flat_left, flat_right, (((0,), (0,)), ((), ())), preferred_element_type=jnp.float32
    )


def gated(gate, lifted):
    return jax.nn.gelu(gate, approximate=True) * lifted


def fetch_attention(first, second, third, fourth):
    return (
        lax.all_gather(first, ("mem", "dp"), axis=0, tiled=True),
        lax.all_gather(second, ("mem", "dp"), axis=0, tiled=True),
        lax.all_gather(third, ("mem", "dp"), axis=0, tiled=True),
        lax.all_gather(fourth, ("mem", "dp"), axis=0, tiled=True),
    )


def fetch_ffn(first, second, third):
    return (
        lax.all_gather(first, ("mem", "dp"), axis=0, tiled=True),
        lax.all_gather(second, ("mem", "dp"), axis=0, tiled=True),
        lax.all_gather(third, ("mem", "dp"), axis=0, tiled=True),
    )


def reduce_attention(first, second, third, fourth):
    return (
        lax.psum_scatter(first, ("mem", "dp"), scatter_dimension=0, tiled=True),
        lax.psum_scatter(second, ("mem", "dp"), scatter_dimension=0, tiled=True),
        lax.psum_scatter(third, ("mem", "dp"), scatter_dimension=0, tiled=True),
        lax.psum_scatter(fourth, ("mem", "dp"), scatter_dimension=0, tiled=True),
    )


def reduce_ffn(first, second, third):
    return (
        lax.psum_scatter(first, ("mem", "dp"), scatter_dimension=0, tiled=True),
        lax.psum_scatter(second, ("mem", "dp"), scatter_dimension=0, tiled=True),
        lax.psum_scatter(third, ("mem", "dp"), scatter_dimension=0, tiled=True),
    )


def cross_pairs(local_memory, pair_weight):
    local_pair = project(local_memory, pair_weight).astype(jnp.bfloat16)
    return lax.all_to_all(local_pair, "mem", split_axis=0, concat_axis=1, tiled=True)


def offset_places(start, size, span):
    return start + size - 1 - lax.iota(jnp.int32, size + span)


def score_block(block, keys, start, query_seg, key_seg, bias_info):
    size = block.shape[0]
    heads_kv = block.shape[1]
    groups = block.shape[2]
    span = keys.shape[0]
    scores = jnp.einsum("qkgd,skd->kgqs", block, keys, preferred_element_type=jnp.float32)
    scores = scores * (1.0 / math.sqrt(block.shape[3]))
    allowed = query_seg[:, None] == key_seg[None, :]
    if bias_info is not None:
        distance_bias = bias_info[0]
        heads = distance_bias.shape[0]
        total = size + span
        places = start + lax.iota(jnp.int32, size)
        offset = places[:, None] - lax.iota(jnp.int32, span)[None, :]
        allowed = allowed & (offset >= 0)
        along = jnp.take(
            distance_bias, jnp.clip(offset_places(start, size, span), 0, span - 1), axis=1
        )
        tiled = jnp.tile(along, (1, size))[:, : size * (total - 1)].reshape(heads, size, total - 1)
        extra = tiled[:, :, size - 1 : size - 1 + span]
        scores = scores + extra.reshape(heads_kv, groups, size, span)
    return jnp.where(allowed, scores, NEGATIVE)


def attend_row(queries, keys, values, query_seg, key_seg, bias_info):
    length = queries.shape[0]

    def one_block(pieces):
        block, start = pieces
        scores = score_block(block, keys, start, query_seg, key_seg, bias_info)
        top = jnp.max(scores, axis=-1, keepdims=True)
        expo = jnp.exp(scores - top)
        total = jnp.sum(expo, axis=-1, keepdims=True)
        weights = (expo / total).astype(jnp.bfloat16)
        mixed = jnp.einsum("kgqs,skd->qkgd", weights, values, preferred_element_type=jnp.float32)
        return (mixed, (top + jnp.log(total))[..., 0])

    blocks = queries.reshape((length // length, length) + queries.shape[1:])
    starts = lax.iota(jnp.int32, length // length) * length
    mixed, logsum = lax.map(one_block, (blocks, starts))
    return (mixed.reshape(queries.shape), logsum)


def attend_row_back(queries, keys, values, query_seg, key_seg, bias_info, logsum, mixed_grad):
    length = queries.shape[0]
    count = length // length
    span = keys.shape[0]
    scale = 1.0 / math.sqrt(queries.shape[3])
    heads = queries.shape[1] * queries.shape[2]
    bias_width = 1 if bias_info is None else bias_info[2]

    def one_block(carry, pieces):
        key_total, value_total, bias_total = carry
        block, grad_block, lse_block, start = pieces
        scores = score_block(block, keys, start, query_seg, key_seg, bias_info)
        probs = jnp.exp(scores - lse_block[..., None])
        value_total = value_total + jnp.einsum(
            "kgqs,qkgd->skd",
            probs.astype(jnp.bfloat16),
            grad_block,
            preferred_element_type=jnp.float32,
        )
        prob_grad = jnp.einsum(
            "qkgd,skd->kgqs", grad_block, values, preferred_element_type=jnp.float32
        )
        delta = jnp.sum(probs * prob_grad, axis=-1, keepdims=True)
        score_grad = (probs * (prob_grad - delta)).astype(jnp.bfloat16)
        query_grad = (
            jnp.einsum("kgqs,skd->qkgd", score_grad, keys, preferred_element_type=jnp.float32)
            * scale
        )
        key_total = (
            key_total
            + jnp.einsum("kgqs,qkgd->skd", score_grad, block, preferred_element_type=jnp.float32)
            * scale
        )
        if bias_info is not None:
            total = length + span
            spread = score_grad.astype(jnp.float32).reshape(heads, length, span)
            spread = jnp.pad(spread, ((0, 0), (0, 0), (length - 1, 0))).reshape(
                heads, length * (total - 1)
            )
            spread = jnp.pad(spread, ((0, 0), (0, length))).reshape(heads, length, total)
            diagonal = jnp.sum(spread, axis=1)
            bucket_of = jnp.take(
                bias_info[1], jnp.clip(offset_places(start, length, span), 0, span - 1)
            )
            picker = (bucket_of[:, None] == lax.iota(jnp.int32, bias_width)[None, :]).astype(
                jnp.float32
            )
            bias_total = bias_total + jnp.dot(diagonal, picker, precision=HIGHEST)
        return ((key_total, value_total, bias_total), query_grad)

    blocks = queries.reshape((count, length) + queries.shape[1:])
    grad_blocks = mixed_grad.reshape((count, length) + queries.shape[1:])
    starts = lax.iota(jnp.int32, count) * length
    start_carry = (
        jnp.zeros(keys.shape, jnp.float32),
        jnp.zeros(values.shape, jnp.float32),
        jnp.zeros((heads, bias_width), jnp.float32),
    )
    totals, query_grad = lax.scan(one_block, start_carry, (blocks, grad_blocks, logsum, starts))
    return (query_grad.reshape(queries.shape), totals[0], totals[1], totals[2])


def shards(
    block_input,
    memory,
    out_grad,
    decoder_segments,
    encoder_segments,
    distance_buckets,
    self_gain,
    cross_gain,
    ffn_gain,
    position_bias,
    self_query,
    self_key,
    self_value,
    self_out,
    cross_query,
    cross_key,
    cross_value,
    cross_out,
    ffn_gate,
    ffn_up,
    ffn_down,
):
    rows = block_input.shape[1]
    length = block_input.shape[2]
    width = block_input.shape[3]
    span = encoder_segments.shape[2]
    heads_kv = self_key.shape[1] // DH
    groups = self_query.shape[1] // self_key.shape[1]
    key_cols = self_key.shape[1]
    bucket_count = position_bias.shape[0]
    row_shape = (rows, length, heads_kv, groups, DH)
    stream = block_input.reshape(rows, length, width).astype(jnp.float32)
    local_memory = memory.reshape(memory.shape[1], memory.shape[2], width)
    query_seg = decoder_segments.reshape(rows, length)
    key_seg = encoder_segments.reshape(rows, span)
    one_hot = (distance_buckets[:, None] == lax.iota(jnp.int32, bucket_count)[None, :]).astype(
        jnp.float32
    )
    distance_bias = jnp.dot(one_hot, position_bias, precision=HIGHEST).T
    bias_info = (distance_bias, distance_buckets, bucket_count)

    def self_forward(pieces):
        return attend_row(pieces[0], pieces[1], pieces[2], pieces[3], pieces[3], bias_info)

    def cross_forward(pieces):
        return attend_row(pieces[0], pieces[1], pieces[2], pieces[3], pieces[4], None)

    def self_backward(pieces):
        return attend_row_back(
            pieces[0], pieces[1], pieces[2], pieces[3], pieces[3], bias_info, pieces[4], pieces[5]
        )

    def cross_backward(pieces):
        return attend_row_back(
            pieces[0], pieces[1], pieces[2], pieces[3], pieces[4], None, pieces[5], pieces[6]
        )

    self_weights = fetch_attention(self_query, self_key, self_value, self_out)
    normed, self_scale = norm_rows(stream, self_gain)
    self_normed = normed.astype(jnp.bfloat16)
    self_queries = project(self_normed, self_weights[0]).astype(jnp.bfloat16).reshape(row_shape)
    self_keys = (
        project(self_normed, self_weights[1])
        .astype(jnp.bfloat16)
        .reshape(rows, length, heads_kv, DH)
    )
    self_values = (
        project(self_normed, self_weights[2])
        .astype(jnp.bfloat16)
        .reshape(rows, length, heads_kv, DH)
    )
    self_mixed, self_logsum = lax.map(
        self_forward, (self_queries, self_keys, self_values, query_seg)
    )
    self_mixed = self_mixed.reshape(rows, length, -1).astype(jnp.bfloat16)
    middle = stream + project_back(self_mixed, self_weights[3])
    cross_weights = fetch_attention(cross_query, cross_key, cross_value, cross_out)
    normed, cross_scale = norm_rows(middle, cross_gain)
    cross_normed = normed.astype(jnp.bfloat16)
    cross_queries = project(cross_normed, cross_weights[0]).astype(jnp.bfloat16).reshape(row_shape)
    pair_weight = jnp.concatenate([cross_weights[1], cross_weights[2]], axis=1)
    pair = cross_pairs(local_memory, pair_weight)
    cross_keys = pair[..., :key_cols].reshape(rows, span, heads_kv, DH)
    cross_values = pair[..., key_cols:].reshape(rows, span, heads_kv, DH)
    cross_mixed, cross_logsum = lax.map(
        cross_forward, (cross_queries, cross_keys, cross_values, query_seg, key_seg)
    )
    cross_mixed = cross_mixed.reshape(rows, length, -1).astype(jnp.bfloat16)
    second = middle + project_back(cross_mixed, cross_weights[3])
    ffn_weights = fetch_ffn(ffn_gate, ffn_up, ffn_down)
    normed, ffn_scale = norm_rows(second, ffn_gain)
    ffn_normed = normed.astype(jnp.bfloat16)
    gate = project(ffn_normed, ffn_weights[0])
    lifted = project(ffn_normed, ffn_weights[1])
    hidden = gated(gate, lifted).astype(jnp.bfloat16)
    result = second + project_back(hidden, ffn_weights[2])
    grad = out_grad.reshape(rows, length, width).astype(jnp.float32)
    ffn_back = fetch_ffn(ffn_gate, ffn_up, ffn_down)
    branch_grad = grad.astype(jnp.bfloat16)
    down_grad = weight_grad(branch_grad, hidden)
    hidden_grad = project(branch_grad, ffn_back[2])
    unused, gated_back = jax.vjp(gated, gate, lifted)
    gate_grad, lifted_grad = gated_back(hidden_grad)
    gate_grad = gate_grad.astype(jnp.bfloat16)
    lifted_grad = lifted_grad.astype(jnp.bfloat16)
    gate_weight_grad = weight_grad(ffn_normed, gate_grad)
    lifted_weight_grad = weight_grad(ffn_normed, lifted_grad)
    normed_grad = project_back(gate_grad, ffn_back[0]) + project_back(lifted_grad, ffn_back[1])
    stream_grad, ffn_gain_grad = norm_back(second, ffn_scale, ffn_gain, normed_grad)
    grad = grad + stream_grad
    ffn_grads = reduce_ffn(gate_weight_grad, lifted_weight_grad, down_grad)
    cross_back = fetch_attention(cross_query, cross_key, cross_value, cross_out)
    pair_back = jnp.concatenate([cross_back[1], cross_back[2]], axis=1)
    pair_again = cross_pairs(local_memory, pair_back)
    keys_again = pair_again[..., :key_cols].reshape(rows, span, heads_kv, DH)
    values_again = pair_again[..., key_cols:].reshape(rows, span, heads_kv, DH)
    branch_grad = grad.astype(jnp.bfloat16)
    cross_out_grad = weight_grad(branch_grad, cross_mixed)
    mixed_grad = project(branch_grad, cross_back[3]).astype(jnp.bfloat16).reshape(row_shape)
    query_grad, key_grad, value_grad, unused = lax.map(
        cross_backward,
        (cross_queries, keys_again, values_again, query_seg, key_seg, cross_logsum, mixed_grad),
    )
    query_low = query_grad.reshape(rows, length, -1).astype(jnp.bfloat16)
    pair_grad = jnp.concatenate(
        [key_grad.reshape(rows, span, -1), value_grad.reshape(rows, span, -1)], axis=-1
    ).astype(jnp.bfloat16)
    cross_query_grad = weight_grad(cross_normed, query_low)
    normed_grad = project_back(query_low, cross_back[0])
    local_grad = lax.all_to_all(pair_grad, "mem", split_axis=1, concat_axis=0, tiled=True)
    pair_weight_grad = weight_grad(local_memory, local_grad)
    memory_grad = project_back(local_grad, pair_back)
    stream_grad, cross_gain_grad = norm_back(middle, cross_scale, cross_gain, normed_grad)
    grad = grad + stream_grad
    cross_grads = reduce_attention(
        cross_query_grad,
        pair_weight_grad[:, :key_cols],
        pair_weight_grad[:, key_cols:],
        cross_out_grad,
    )
    self_back = fetch_attention(self_query, self_key, self_value, self_out)
    branch_grad = grad.astype(jnp.bfloat16)
    self_out_grad = weight_grad(branch_grad, self_mixed)
    mixed_grad = project(branch_grad, self_back[3]).astype(jnp.bfloat16).reshape(row_shape)
    query_grad, key_grad, value_grad, distance_grad = lax.map(
        self_backward, (self_queries, self_keys, self_values, query_seg, self_logsum, mixed_grad)
    )
    query_low = query_grad.reshape(rows, length, -1).astype(jnp.bfloat16)
    key_low = key_grad.reshape(rows, length, -1).astype(jnp.bfloat16)
    value_low = value_grad.reshape(rows, length, -1).astype(jnp.bfloat16)
    self_query_grad = weight_grad(self_normed, query_low)
    self_key_grad = weight_grad(self_normed, key_low)
    self_value_grad = weight_grad(self_normed, value_low)
    normed_grad = (
        project_back(query_low, self_back[0])
        + project_back(key_low, self_back[1])
        + project_back(value_low, self_back[2])
    )
    stream_grad, self_gain_grad = norm_back(stream, self_scale, self_gain, normed_grad)
    input_grad = grad + stream_grad
    self_grads = reduce_attention(self_query_grad, self_key_grad, self_value_grad, self_out_grad)
    table_grad = jnp.sum(distance_grad, axis=0).T
    small = lax.psum((self_gain_grad, cross_gain_grad, ffn_gain_grad, table_grad), ("mem", "dp"))
    return (
        result.astype(jnp.bfloat16).reshape(block_input.shape),
        input_grad.reshape(block_input.shape),
        memory_grad.reshape(memory.shape),
        small[0],
        small[1],
        small[2],
        small[3],
        self_grads[0],
        self_grads[1],
        self_grads[2],
        self_grads[3],
        cross_grads[0],
        cross_grads[1],
        cross_grads[2],
        cross_grads[3],
        ffn_grads[0],
        ffn_grads[1],
        ffn_grads[2],
    )


def solution(mesh):
    in_specs = (
        P("dp", "mem", None, None),
        P("dp", None, "mem", None),
        P("dp", "mem", None, None),
        P("dp", "mem", None),
        P("dp", "mem", None),
        P(),
        P(),
        P(),
        P(),
        P(),
        P(("mem", "dp"), None),
        P(("mem", "dp"), None),
        P(("mem", "dp"), None),
        P(("mem", "dp"), None),
        P(("mem", "dp"), None),
        P(("mem", "dp"), None),
        P(("mem", "dp"), None),
        P(("mem", "dp"), None),
        P(("mem", "dp"), None),
        P(("mem", "dp"), None),
        P(("mem", "dp"), None),
    )
    out_specs = (
        P("dp", "mem", None, None),
        P("dp", "mem", None, None),
        P("dp", None, "mem", None),
        P(),
        P(),
        P(),
        P(),
        P(("mem", "dp"), None),
        P(("mem", "dp"), None),
        P(("mem", "dp"), None),
        P(("mem", "dp"), None),
        P(("mem", "dp"), None),
        P(("mem", "dp"), None),
        P(("mem", "dp"), None),
        P(("mem", "dp"), None),
        P(("mem", "dp"), None),
        P(("mem", "dp"), None),
        P(("mem", "dp"), None),
    )
    return jax.shard_map(shards, mesh=mesh, in_specs=in_specs, out_specs=out_specs, check_vma=False)
```

profile of v0, /device:TPU:0, one launch (start us, length us, event | category | flops | bytes accessed | tf_op | source)
XLA Modules:
  0.0 2292.6 jit_solution(7206812481181635004)
XLA Ops:
  16.9 50.4 %all-gather.20.cloned.1.call-done = bf16[1024,512]{1,0:T(8,128)(2,1)} async-done(((bf16[32,512]{1,0:T(8,128)(2,1)}), bf16[1024,512]{1,0:T(8,128)(2,1)}) %all-gather.20.cloned.1.call-update) | async-done | bytes 1048592 | tf_op jit(solution)/shard_map/all_gather | solution.py:52
  68.8 54.0 %all-gather.22.cloned.1.call-done = bf16[1024,512]{1,0:T(8,128)(2,1)} async-done(((bf16[32,512]{1,0:T(8,128)(2,1)}), bf16[1024,512]{1,0:T(8,128)(2,1)}) %all-gather.22.cloned.1.call-update) | async-done | bytes 1048592 | tf_op jit(solution)/shard_map/all_gather | solution.py:53
  126.6 3.6 all-to-all-start
  131.5 4.9 copy.180
  136.3 3.8 slice.40
  140.1 12.0 reshape.676
  152.1 6.0 slice.41
  158.1 5.4 copy.130
  165.2 22.2 all-gather.14.cloned.1.call-done
  189.3 53.5 %all-gather.12.cloned.1.call-done = bf16[1024,512]{1,0:T(8,128)(2,1)} async-done(((bf16[32,512]{1,0:T(8,128)(2,1)}), bf16[1024,512]{1,0:T(8,128)(2,1)}) %all-gather.12.cloned.1.call-update) | async-done | bytes 1048592 | tf_op jit(solution)/shard_map/all_gather | solution.py:53
  249.5 51.3 %all-gather.16.cloned.1.call-done = bf16[1024,1024]{1,0:T(8,128)(2,1)} async-done(((bf16[32,1024]{1,0:T(8,128)(2,1)}), bf16[1024,1024]{1,0:T(8,128)(2,1)}) %all-gather.16.cloned.1.call-update) | async-done | bytes 2097168 | tf_op jit(solution)/shard_map/all_gather | solution.py:51
  303.4 3.3 fusion.96
  310.3 48.5 %all-gather.18.cloned.1.call-done = bf16[1024,1024]{1,0:T(8,128)(2,1)} async-done(((bf16[32,1024]{1,0:T(8,128)(2,1)}), bf16[1024,1024]{1,0:T(8,128)(2,1)}) %all-gather.18.cloned.1.call-update) | async-done | bytes 2097168 | tf_op jit(solution)/shard_map/all_gather | solution.py:54
  358.8 2.6 multiply_reduce_fusion.5
  361.5 55.5 %all-gather.24.cloned.1.call-done = bf16[1024,1024]{1,0:T(8,128)(2,1)} async-done(((bf16[32,1024]{1,0:T(8,128)(2,1)}), bf16[1024,1024]{1,0:T(8,128)(2,1)}) %all-gather.24.cloned.1.call-update) | async-done | bytes 2097168 | tf_op jit(solution)/shard_map/all_gather | solution.py:51
  416.9 3.1 convolution_convert_fusion.3
  430.2 44.8 %all-gather.26.cloned.1.call-done = bf16[1024,1024]{1,0:T(8,128)(2,1)} async-done(((bf16[32,1024]{1,0:T(8,128)(2,1)}), bf16[1024,1024]{1,0:T(8,128)(2,1)}) %all-gather.26.cloned.1.call-update) | async-done | bytes 2097168 | tf_op jit(solution)/shard_map/all_gather | solution.py:54
  475.0 2.6 multiply_reduce_fusion.4
  479.6 64.5 %all-gather.30.cloned.1.call-done = bf16[1024,2816]{1,0:T(8,128)(2,1)} async-done(((bf16[32,2816]{1,0:T(8,128)(2,1)}), bf16[1024,2816]{1,0:T(8,128)(2,1)}) %all-gather.30.cloned.1.call-update) | async-done | bytes 5767184 | tf_op jit(solution)/shard_map/all_gather | solution.py:61
  544.0 6.1 fusion.100
  550.1 62.9 %all-gather.28.cloned.1.call-done = bf16[1024,2816]{1,0:T(8,128)(2,1)} async-done(((bf16[32,2816]{1,0:T(8,128)(2,1)}), bf16[1024,2816]{1,0:T(8,128)(2,1)}) %all-gather.28.cloned.1.call-update) | async-done | bytes 5767184 | tf_op jit(solution)/shard_map/all_gather | solution.py:60
  613.0 6.2 fusion.99
  619.2 62.9 %all-gather.32.cloned.1.call-done = bf16[1024,2816]{1,0:T(8,128)(2,1)} async-done(((bf16[32,2816]{1,0:T(8,128)(2,1)}), bf16[1024,2816]{1,0:T(8,128)(2,1)}) %all-gather.32.cloned.1.call-update) | async-done | bytes 5767184 | tf_op jit(solution)/shard_map/all_gather | solution.py:62
  682.1 8.9 multiply_convert_fusion
  693.0 4.7 multiply_reduce_fusion
  702.6 5.8 fusion
  719.0 3.0 fusion.50
  724.0 3.4 fusion.7
  733.4 5.7 fusion.42
  739.0 3.9 copy.148
  742.9 4.4 fusion.41
  749.8 4.8 fusion.98
  755.1 8.0 reduce.18
  765.1 32.2 %all_to_all.14 = bf16[4,2,65536]{2,1,0:T(2,128)(2,1)S(1)} all-to-all(bf16[4,2,65536]{2,1,0:T(2,128)(2,1)} %reshape.727), channel_id=1, replica_groups=mesh['mem'=4,'dp'=8] {'mem'}, dimensions={0} | all-to-all | bytes 2097152 | tf_op jit(solution)/shard_map/all_to_all | solution.py:327
  806.2 2.9 copy.174
  809.1 3.0 copy.172
  812.3 3.8 fusion.75
  817.1 2.8 fusion.84
  820.0 4.2 fusion.72
  826.5 3.9 fusion.89
  830.5 7.4 convolution_bitcast_fusion
  837.9 11.9 copy.176
  849.9 7.5 fusion.104
  857.4 7.4 fusion.103
  865.5 3.7 gather_fusion
  871.6 4.8 pad.14
  876.4 8.8 reshape.684
  885.3 2.7 pad_convert_fusion
  888.0 4.9 copy.181
  892.9 2.5 bitcast_reduce_fusion
  898.7 38.6 %all-reduce.2 = (f32[1024]{0:T(1024)}, f32[1024]{0:T(1024)}, f32[1024]{0:T(1024)}, f32[32,16]{0,1:T(8,128)}) all-reduce(f32[1024]{0:T(1024)S(1)} %get-tuple-element.375, f32[1024]{0:T(1024)S(1)} %get-tuple-element.373, f32[1024]{0:T(1024)S(1)} %get-tuple-element.371, ...), channel_id=1, replica_groups=mesh['mem'=4,'dp'=8] {'mem','dp'}, use_global_device_ids=true, to_apply=%region_13.15 | all-reduce | flops 3584 | bytes 28672 | tf_op jit(solution)/shard_map/psum | solution.py:360
  937.3 2.5 fusion.59
  939.8 6.0 fusion.49
  945.8 2.6 convolution_bitcast_fusion.2
  948.4 48.5 %reduce-scatter.20.cloned.1.call-done = f32[32,512]{1,0:T(8,128)} async-done(((f32[1024,512]{1,0:T(8,128)}), f32[32,512]{1,0:T(8,128)}) %reduce-scatter.20.cloned.1.call-update) | async-done | bytes 65552 | tf_op jit(solution)/shard_map/reduce_scatter | solution.py:69
  996.8 134.9 %reduce-scatter.36.cloned.1.call-done = f32[32,512]{1,0:T(8,128)} async-done(((f32[1024,512]{1,0:T(8,128)}), f32[32,512]{1,0:T(8,128)}) %reduce-scatter.36.cloned.1.call-update) | async-done | bytes 65552
  1131.8 135.0 %reduce-scatter.34.cloned.1.call-done = f32[32,512]{1,0:T(8,128)} async-done(((f32[1024,512]{1,0:T(8,128)}), f32[32,512]{1,0:T(8,128)}) %reduce-scatter.34.cloned.1.call-update) | async-done | bytes 65552
  1266.7 139.3 %reduce-scatter.28.cloned.1.call-done = f32[32,1024]{1,0:T(8,128)} async-done(((f32[1024,1024]{1,0:T(8,128)}), f32[32,1024]{1,0:T(8,128)}) %reduce-scatter.28.cloned.1.call-update) | async-done | bytes 131088 | tf_op jit(solution)/shard_map/reduce_scatter | solution.py:71
  1406.1 139.3 %reduce-scatter.26.cloned.1.call-done = f32[32,1024]{1,0:T(8,128)} async-done(((f32[1024,1024]{1,0:T(8,128)}), f32[32,1024]{1,0:T(8,128)}) %reduce-scatter.26.cloned.1.call-update) | async-done | bytes 131088 | tf_op jit(solution)/shard_map/reduce_scatter | solution.py:68
  1545.4 139.4 %reduce-scatter.24.cloned.1.call-done = f32[32,1024]{1,0:T(8,128)} async-done(((f32[1024,1024]{1,0:T(8,128)}), f32[32,1024]{1,0:T(8,128)}) %reduce-scatter.24.cloned.1.call-update) | async-done | bytes 131088 | tf_op jit(solution)/shard_map/reduce_scatter | solution.py:71
  1684.8 139.7 %reduce-scatter.18.cloned.1.call-done = f32[32,1024]{1,0:T(8,128)} async-done(((f32[1024,1024]{1,0:T(8,128)}), f32[32,1024]{1,0:T(8,128)}) %reduce-scatter.18.cloned.1.call-update) | async-done | bytes 131088 | tf_op jit(solution)/shard_map/reduce_scatter | solution.py:68
  1824.4 153.6 %reduce-scatter.38.cloned.1.call-done = f32[32,2816]{1,0:T(8,128)} async-done(((f32[1024,2816]{1,0:T(8,128)}), f32[32,2816]{1,0:T(8,128)}) %reduce-scatter.38.cloned.1.call-update) | async-done | bytes 360464
  1978.0 153.7 %reduce-scatter.32.cloned.1.call-done = f32[32,2816]{1,0:T(8,128)} async-done(((f32[1024,2816]{1,0:T(8,128)}), f32[32,2816]{1,0:T(8,128)}) %reduce-scatter.32.cloned.1.call-update) | async-done | bytes 360464 | tf_op jit(solution)/shard_map/reduce_scatter | solution.py:78
  2131.6 153.7 %reduce-scatter.30.cloned.1.call-done = f32[32,2816]{1,0:T(8,128)} async-done(((f32[1024,2816]{1,0:T(8,128)}), f32[32,2816]{1,0:T(8,128)}) %reduce-scatter.30.cloned.1.call-update) | async-done | bytes 360464 | tf_op jit(solution)/shard_map/reduce_scatter | solution.py:77
  (237 shorter events, 93.4 us)
Async XLA Ops:
  7.2 117.1 %copy-start = (bf16[1,4,128,1024]{3,2,1,0:T(8,128)(2,1)S(1)}, bf16[1,4,128,1024]{3,2,1,0:T(8,128)(2,1)}, u32[]{:S(2)}) copy-start(bf16[1,4,128,1024]{3,2,1,0:T(8,128)(2,1)} %param.24) | copy-start | bytes 3145732
  7.2 60.1 %all-gather.20.cloned.1.call-start = ((), (), s32[]{:S(2)}) async-start(), calls=%async_computation.17 | async-start | bytes 1081344 | tf_op jit(solution)/shard_map/all_gather | solution.py:52
  7.9 114.9 %all-gather.22.cloned.1.call-start = ((), (), s32[]{:S(2)}) async-start(), calls=%async_computation.18 | async-start | bytes 1081344 | tf_op jit(solution)/shard_map/all_gather | solution.py:53
  8.7 178.7 %all-gather.14.cloned.1.call-start = ((), (), s32[]{:S(2)}) async-start(), calls=%async_computation.14 | async-start | bytes 1081344 | tf_op jit(solution)/shard_map/all_gather | solution.py:52
  9.4 233.3 %all-gather.12.cloned.1.call-start = ((), (), s32[]{:S(2)}) async-start(), calls=%async_computation.13 | async-start | bytes 1081344 | tf_op jit(solution)/shard_map/all_gather | solution.py:53
  10.0 290.8 %all-gather.16.cloned.1.call-start = ((), (), s32[]{:S(2)}) async-start(), calls=%async_computation.15 | async-start | bytes 2162688 | tf_op jit(solution)/shard_map/all_gather | solution.py:51
  10.6 348.2 %all-gather.18.cloned.1.call-start = ((), (), s32[]{:S(2)}) async-start(), calls=%async_computation.16 | async-start | bytes 2162688 | tf_op jit(solution)/shard_map/all_gather | solution.py:54
  11.2 405.8 %all-gather.24.cloned.1.call-start = ((), (), s32[]{:S(2)}) async-start(), calls=%async_computation.19 | async-start | bytes 2162688 | tf_op jit(solution)/shard_map/all_gather | solution.py:51
  11.9 463.1 %all-gather.26.cloned.1.call-start = ((), (), s32[]{:S(2)}) async-start(), calls=%async_computation.20 | async-start | bytes 2162688 | tf_op jit(solution)/shard_map/all_gather | solution.py:54
  12.7 531.4 %all-gather.30.cloned.1.call-start = ((), (), s32[]{:S(2)}) async-start(), calls=%async_computation.22 | async-start | bytes 5947392 | tf_op jit(solution)/shard_map/all_gather | solution.py:61
  13.4 599.6 %all-gather.28.cloned.1.call-start = ((), (), s32[]{:S(2)}) async-start(), calls=%async_computation.21 | async-start | bytes 5947392 | tf_op jit(solution)/shard_map/all_gather | solution.py:60
  14.0 668.1 %all-gather.32.cloned.1.call-start = ((), (), s32[]{:S(2)}) async-start(), calls=%async_computation.23 | async-start | bytes 5947392 | tf_op jit(solution)/shard_map/all_gather | solution.py:62
  68.8 57.8 %copy-start.41 = (bf16[1024,512]{0,1:T(8,128)(2,1)}, bf16[1024,512]{0,1:T(8,128)(2,1)S(1)}, u32[]{:S(2)}) copy-start(bf16[1024,512]{0,1:T(8,128)(2,1)S(1)} %copy.132) | copy-start | bytes 3145732
  126.6 118.7 %all-to-all-start = ((bf16[4,128,1024]{1,2,0:T(8,128)(2,1)}), bf16[4,128,1024]{1,2,0:T(8,128)(2,1)S(1)}, u32[]{:S(2)}, u32[]{:S(2)}) async-start(bf16[4,128,1024]{1,2,0:T(8,128)(2,1)} %fusion.31), calls=%async_computation | async-start | bytes 2097152 | tf_op jit(solution)/shard_map/all_to_all | solution.py:85
  130.1 818.3 %reduce-scatter.22.cloned.1.call-start = ((), (), s32[]{:S(2)}) async-start(), calls=%async_computation.26 | async-start | bytes 2162688 | tf_op jit(solution)/shard_map/reduce_scatter | solution.py:70
  158.1 5.5 copy-start.8
  158.1 6.2 copy-start.54
  158.1 7.0 copy-start.56
  158.1 29.3 %copy-start.45 = (f32[1024]{0:T(1024)S(1)}, f32[1024]{0:T(1024)}, u32[]{:S(2)}) copy-start(f32[1024]{0:T(1024)} %param.29) | copy-start | bytes 12292
  164.3 136.5 %copy-start.51 = (f32[256]{0:T(256)}, f32[256]{0:T(256)S(1)}, u32[]{:S(2)}) copy-start(f32[256]{0:T(256)S(1)} %get-tuple-element.389) | copy-start | bytes 3076
  189.2 114.2 %copy-start.30 = (bf16[256,512]{0,1:T(8,128)(2,1)}, bf16[256,512]{0,1:T(8,128)(2,1)S(1)}, u32[]{:S(2)}) copy-start(bf16[256,512]{0,1:T(8,128)(2,1)S(1)} %copy.126) | copy-start | bytes 786436
  303.4 3.3 copy-start.28
  310.3 106.6 %copy-start.47 = (f32[1024]{0:T(1024)S(1)}, f32[1024]{0:T(1024)}, u32[]{:S(2)}) copy-start(f32[1024]{0:T(1024)} %param.30) | copy-start | bytes 12292
  361.4 353.5 %copy-start.49 = (f32[256]{0:T(256)}, f32[256]{0:T(256)S(1)}, u32[]{:S(2)}) copy-start(f32[256]{0:T(256)S(1)} %get-tuple-element.391) | copy-start | bytes 3076
  424.5 3.3 copy-start.2
  424.5 3.3 copy-start.34
  430.2 48.4 %copy-start.53 = (f32[1024]{0:T(1024)S(1)}, f32[1024]{0:T(1024)}, u32[]{:S(2)}) copy-start(f32[1024]{0:T(1024)} %param.31) | copy-start | bytes 12292
  682.1 8.9 copy-start.57
  693.0 4.7 copy-start.35
  693.0 6.0 copy-start.18
  702.6 5.8 slice-start
  702.6 6.2 slice-start.1
  710.8 3.1 copy-start.19
  712.9 2.3 copy-start.20
  713.9 2.3 copy-start.17
  716.2 5.8 copy-start.46
  716.2 5.8 copy-start.52
  723.9 272.9 %reduce-scatter.20.cloned.1.call-start = ((), (), s32[]{:S(2)}) async-start(), calls=%async_computation.25 | async-start | bytes 2162688 | tf_op jit(solution)/shard_map/reduce_scatter | solution.py:69
  724.0 3.5 copy-start.4
  727.5 2.3 copy-start.29
  729.8 3.5 copy-start.25
  733.3 9.7 copy-start.24
  733.3 398.5 %reduce-scatter.36.cloned.1.call-start = ((), (), s32[]{:S(2)}) async-start(), calls=%async_computation.33 | async-start | bytes 2162688
  809.1 3.2 copy-start.14
  809.1 457.6 %reduce-scatter.34.cloned.1.call-start = ((), (), s32[]{:S(2)}) async-start(), calls=%async_computation.32 | async-start | bytes 2162688
  812.2 3.9 copy-start.48
  812.2 3.9 copy-start.50
  812.2 593.9 %reduce-scatter.28.cloned.1.call-start = ((), (), s32[]{:S(2)}) async-start(), calls=%async_computation.29 | async-start | bytes 4325376 | tf_op jit(solution)/shard_map/reduce_scatter | solution.py:71
  816.1 729.3 %reduce-scatter.26.cloned.1.call-start = ((), (), s32[]{:S(2)}) async-start(), calls=%async_computation.28 | async-start | bytes 4325376 | tf_op jit(solution)/shard_map/reduce_scatter | solution.py:68
  819.9 4.3 copy-start.7
  819.9 864.8 %reduce-scatter.24.cloned.1.call-start = ((), (), s32[]{:S(2)}) async-start(), calls=%async_computation.27 | async-start | bytes 4325376 | tf_op jit(solution)/shard_map/reduce_scatter | solution.py:71
  824.2 1000.2 %reduce-scatter.18.cloned.1.call-start = ((), (), s32[]{:S(2)}) async-start(), calls=%async_computation.24 | async-start | bytes 4325376 | tf_op jit(solution)/shard_map/reduce_scatter | solution.py:68
  830.4 1147.6 %reduce-scatter.38.cloned.1.call-start = ((), (), s32[]{:S(2)}) async-start(), calls=%async_computation.34 | async-start | bytes 11894784
  849.8 1281.8 %reduce-scatter.32.cloned.1.call-start = ((), (), s32[]{:S(2)}) async-start(), calls=%async_computation.31 | async-start | bytes 11894784 | tf_op jit(solution)/shard_map/reduce_scatter | solution.py:78
  857.4 1428.0 %reduce-scatter.30.cloned.1.call-start = ((), (), s32[]{:S(2)}) async-start(), calls=%async_computation.30 | async-start | bytes 11894784 | tf_op jit(solution)/shard_map/reduce_scatter | solution.py:77
  892.9 2.8 copy-start.27
  892.9 2.8 copy-start.33
  892.9 3.6 copy-start.32
  892.9 3.6 copy-start.40
  896.5 40.8 %copy-start.11 = (f32[256,1024]{1,0:T(8,128)S(1)}, f32[256,1024]{1,0:T(8,128)}, u32[]{:S(2)}) copy-start(f32[256,1024]{1,0:T(8,128)} %copy-done.10) | copy-start | bytes 3145732
  896.5 40.8 %copy-start.55 = (f32[256]{0:T(256)S(1)}, f32[256]{0:T(256)}, u32[]{:S(2)}) copy-start(f32[256]{0:T(256)} %get-tuple-element.388) | copy-start | bytes 3076
  939.8 6.0 copy-start.23
  939.8 6.0 copy-start.42
  939.8 6.0 copy-start.44
  (19 other events, 27.5 us)
Sparse Core Ops, SparseCore 0:
  10.9 56.3 all-gather.19
  70.2 52.6 all-gather.21
  125.7 61.6 all-gather.13
  190.1 52.6 all-gather.11
  245.5 55.3 all-gather.15
  303.5 55.2 all-gather.17
  361.7 55.2 all-gather.23
  419.8 55.2 all-gather.25
  477.9 66.1 all-gather.29
  546.7 66.2 all-gather.27
  615.8 66.2 all-gather.31
  724.0 136.9 reduce-scatter.21
  864.0 132.8 reduce-scatter.19
  999.5 132.1 reduce-scatter.35
  1134.5 132.1 reduce-scatter.33
  1269.4 136.5 reduce-scatter.27
  1408.8 136.5 reduce-scatter.25
  1548.1 136.6 reduce-scatter.23
  1687.6 136.7 reduce-scatter.17
  1827.1 150.7 reduce-scatter.37
  1980.9 150.7 reduce-scatter.31
  2134.5 150.7 reduce-scatter.29
where the time goes:
time: 2300 us; the launch traced here: 2290 us
  waiting for transfers between devices  1910 us (83%)
  matrix products  138 us (6%)
  local copies, waits for them, and re-layouts  121 us (5%)
  blocking collectives  70.8 us (3%)
  other arithmetic  28.7 us (1%)
    unnamed x25, waiting for transfers between devices  431 us
    reduce_scatter x2, waiting for transfers between devices, reduce_attention(): lax.psum_scatter(first, ('mem', 'dp'), scatter_dimension=0, tiled=True)  279 us
    reduce_scatter x2, waiting for transfers between devices, reduce_attention(): lax.psum_scatter(fourth, ('mem', 'dp'), scatter_dimension=0, tiled=True)  279 us
    reduce_scatter x1, waiting for transfers between devices, reduce_ffn(): lax.psum_scatter(first, ('mem', 'dp'), scatter_dimension=0, tiled=True)  154 us
    reduce_scatter x1, waiting for transfers between devices, reduce_ffn(): lax.psum_scatter(second, ('mem', 'dp'), scatter_dimension=0, tiled=True)  154 us
    all_gather x2, waiting for transfers between devices, fetch_attention(): lax.all_gather(third, ('mem', 'dp'), axis=0, tiled=True)  108 us
    all_gather x2, waiting for transfers between devices, fetch_attention(): lax.all_gather(first, ('mem', 'dp'), axis=0, tiled=True)  107 us
    all_gather x2, waiting for transfers between devices, fetch_attention(): lax.all_gather(fourth, ('mem', 'dp'), axis=0, tiled=True)  93.3 us
  transfers between devices with their start and end apart: 23, of which 21 were waited for; matrix products, arithmetic and copies ran while one was open for 10% of the time, Pallas kernels for 0%

commit v1 on v0

v1 whole, which is shorter than its diff:
```python
import functools

import jax
import jax.numpy as jnp
import numpy as np
from jax import lax
from jax.experimental import pallas as pl
from jax.experimental.pallas import tpu as pltpu
from jax.sharding import PartitionSpec as P

DH = 64
TILE = 256
EPSILON = 1e-06
NEGATIVE = -1e30
AXES = ("mem", "dp")
F32 = jnp.float32
BF16 = jnp.bfloat16
HIGHEST = lax.Precision.HIGHEST
VMEM = 58 * 1024 * 1024


def steps(n):
    high = list(range(n.bit_length() - 2, 2, -1))
    return (high + [2, 1], high + [1, 2])


def exchange(n, k):
    order = steps(n)
    return [(d, d ^ (1 << order[d & 1][k])) for d in range(n)]


def sibling(n):
    return [(d, d ^ 1) for d in range(n)]


def source(n, me):
    order = steps(n)
    half = n // 2
    table = np.zeros((2, half), np.int32)
    for core in range(2):
        for slot in range(half):
            for k in range(len(order[core])):
                if slot >> k & 1:
                    table[core, slot] ^= 1 << order[core][k]
    odd = (me & 1) == 1
    own = jnp.where(odd, table[1], table[0])
    other = jnp.where(odd, table[0], table[1])
    return jnp.concatenate([me ^ own, me ^ 1 ^ other])


def gather(shard, n):
    held = shard
    last = n.bit_length() - 3
    for k in range(last):
        held = jnp.concatenate([held, lax.ppermute(held, AXES, exchange(n, k))], axis=0)
    pieces = [held, lax.ppermute(held, AXES, exchange(n, last))]
    return pieces + [lax.ppermute(piece, AXES, sibling(n)) for piece in pieces]


def scatter(pieces, n):
    last = n.bit_length() - 3
    there = [lax.ppermute(piece, AXES, sibling(n)) for piece in pieces[2:]]
    send = (pieces[1].astype(F32) + there[1].astype(F32)).astype(BF16)
    held = pieces[0].astype(F32) + there[0].astype(F32)
    held = held + lax.ppermute(send, AXES, exchange(n, last)).astype(F32)
    for k in range(last - 1, -1, -1):
        half = held.shape[0] // 2
        came = lax.ppermute(held[half:].astype(BF16), AXES, exchange(n, k))
        held = held[:half] + came.astype(F32)
    return held


def sum_all(value, n):
    for bit in range(n.bit_length() - 1):
        value = value + lax.ppermute(value, AXES, [(d, d ^ (1 << bit)) for d in range(n)])
    return value


def swap_rows(blocks, nm, nd):
    n = nm * nd
    return [blocks[0]] + [
        lax.ppermute(blocks[t], AXES, [(d, d ^ (t * nd)) for d in range(n)]) for t in range(1, nm)
    ]


def dot(left, right, a=1, b=0):
    return lax.dot_general(left, right, (((a,), (b,)), ((), ())), preferred_element_type=F32)


def rows_of(left, p):
    size = left.shape[1] // 4
    return left[:, p * size : (p + 1) * size]


def project(left, weights):
    total = dot(rows_of(left, 0), weights[0])
    for p in range(1, 4):
        total = total + dot(rows_of(left, p), weights[p])
    return total


def project_back(left, weights):
    return jnp.concatenate([dot(left, w, 1, 1) for w in weights], axis=1)


def scale_of(stream):
    return lax.rsqrt(jnp.mean(stream * stream, axis=1, keepdims=True) + EPSILON)


def norm_back(stream, gain, grad):
    scale = scale_of(stream)
    weighted = grad * gain
    inner = jnp.mean(weighted * stream, axis=1, keepdims=True)
    out = scale * weighted - stream * (scale * scale * scale) * inner
    return out, jnp.sum(grad * stream * scale, axis=0, keepdims=True)


def transposed(value):
    return value.astype(F32).T.astype(BF16)


def spread(part):
    zero = jnp.zeros_like(part)
    top = jnp.concatenate([part, zero], axis=1)
    low = jnp.concatenate([zero, part], axis=1)
    return jnp.concatenate([top, low], axis=0)


def softmax(scores):
    expo = jnp.exp(scores - jnp.max(scores, axis=1, keepdims=True))
    return (expo / jnp.sum(expo, axis=1, keepdims=True)).astype(BF16)


def toeplitz(start):
    block = start
    size = block.shape[0]
    while size < start.shape[1]:
        block = jnp.concatenate([block, pltpu.roll(block, size, 1)], axis=0)
        size *= 2
    return block


def diagonals(block):
    size = block.shape[0]
    while size > 8:
        size //= 2
        block = block[:size] + pltpu.roll(block[size:], block.shape[1] - size, 1)
    return block


def self_forward(x, normed, start, seg_col, seg_row, gain, w0, w1, w2, w3,
                 q_out, kt_out, vt_out, p_out, mixed_out, middle_out, n_out):
    weights = (w0, w1, w2, w3)
    width = x.shape[1]
    keys = w0.shape[1] - 2 * width
    kv = keys // 2
    length = x.shape[0]
    n = normed[...]
    q_out[...] = (project(n, [w[:, :width] for w in weights]).astype(BF16).astype(F32) * 0.125).astype(BF16)
    pair = project(n, [w[:, width : width + keys] for w in weights])
    pair_t = pair.T.astype(BF16)
    kt_out[...] = pair_t[:kv]
    vt_out[...] = pair_t[kv:]
    row = lax.broadcasted_iota(jnp.int32, (length, length), 0)
    column = lax.broadcasted_iota(jnp.int32, (length, length), 1)
    allowed = (column <= row) & (seg_col[...] == seg_row[...])
    for g in range(kv // DH):
        kk = spread(kt_out[g * DH : (g + 1) * DH])
        vv = spread(vt_out[g * DH : (g + 1) * DH])
        scores = dot(q_out[:, g * 2 * DH : (g + 1) * 2 * DH], kk)
        for h in range(2):
            part = scores[:, h * length : (h + 1) * length] + toeplitz(start[2 * g + h])
            p_out[g, :, h * length : (h + 1) * length] = softmax(jnp.where(allowed, part, NEGATIVE))
        mixed_out[:, g * 2 * DH : (g + 1) * 2 * DH] = dot(p_out[g], vv, 1, 1).astype(BF16)
    middle = x[...].astype(F32) + project_back(mixed_out[...], [w[:, width + keys :] for w in weights])
    middle_out[...] = middle
    n_out[...] = (middle * scale_of(middle) * gain[...]).astype(BF16)


def memory_forward(memory, w0, w1, w2, w3, pair_out):
    pair = project(memory[...], [w[...] for w in (w0, w1, w2, w3)])
    pair_out[...] = pair.T.astype(BF16)


def cross_forward(middle, normed, pair, seg_col, seg_row, gain, w0, w1, w2, w3,
                  q_out, p_out, mixed_out, second_out, n_out, nt_out):
    weights = (w0, w1, w2, w3)
    width = middle.shape[1]
    kv = pair.shape[0] // 2
    span = pair.shape[1]
    q = project(normed[...], [w[:, :width] for w in weights])
    q_out[...] = (q.astype(BF16).astype(F32) * 0.125).astype(BF16)
    allowed = seg_col[...] == seg_row[...]
    for g in range(kv // DH):
        kk = spread(pair[g * DH : (g + 1) * DH])
        vv = spread(pair[kv + g * DH : kv + (g + 1) * DH])
        scores = dot(q_out[:, g * 2 * DH : (g + 1) * 2 * DH], kk)
        for h in range(2):
            part = scores[:, h * span : (h + 1) * span]
            p_out[g, :, h * span : (h + 1) * span] = softmax(jnp.where(allowed, part, NEGATIVE))
        mixed_out[:, g * 2 * DH : (g + 1) * 2 * DH] = dot(p_out[g], vv, 1, 1).astype(BF16)
    second = middle[...] + project_back(mixed_out[...], [w[:, width:] for w in weights])
    second_out[...] = second
    n = second * scale_of(second) * gain[...]
    n_out[...] = n.astype(BF16)
    nt_out[...] = n.T.astype(BF16)


def ffn_tile(n, nt, dy, dyt, res_in, dn_in, w0, w1, w2, w3, res_out, dn_out, g0, g1, g2, g3):
    weights = (w0, w1, w2, w3)

    @pl.when(pl.program_id(0) == 0)
    def _():
        res_out[...] = res_in[...]
        dn_out[...] = dn_in[...]

    pair = project(n[...], [w[:, : 2 * TILE] for w in weights])
    gate = pair[:, :TILE]
    lifted = pair[:, TILE:]
    hidden_grad = project(dy[...], [w[:, 2 * TILE :] for w in weights])
    root = 0.7978845608028654
    square = gate * gate
    tanh = jnp.tanh(root * gate * (1.0 + 0.044715 * square))
    half = 0.5 * (1.0 + tanh)
    gelu = gate * half
    slope = half + 0.5 * gate * (1.0 - tanh * tanh) * (root * (1.0 + 3.0 * 0.044715 * square))
    hidden = (gelu * lifted).astype(BF16)
    pair_grad = jnp.concatenate(
        [(hidden_grad * lifted * slope).astype(BF16), (hidden_grad * gelu).astype(BF16)], axis=1
    )
    res_out[...] += project_back(hidden, [w[:, 2 * TILE :] for w in weights])
    dn_out[...] += project_back(pair_grad, [w[:, : 2 * TILE] for w in weights])
    size = n.shape[1] // 4
    for p, g in enumerate((g0, g1, g2, g3)):
        g[:, : 2 * TILE] = dot(nt[p * size : (p + 1) * size], pair_grad).astype(BF16)
        g[:, 2 * TILE :] = dot(dyt[p * size : (p + 1) * size], hidden).astype(BF16)


def ffn_end(second, res, dn, dy, gain, w0, w1, w2, w3, result_out, grad_out, gain_out, branch_out, mixed_out):
    result_out[...] = (second[...] + res[...]).astype(BF16)
    back, gain_grad = norm_back(second[...], gain[...], dn[...])
    grad = dy[...].astype(F32) + back
    grad_out[...] = grad
    gain_out[...] = gain_grad
    branch = grad.astype(BF16)
    branch_out[...] = branch
    mixed_out[...] = project(branch, [w[...] for w in (w0, w1, w2, w3)]).astype(BF16)


def attention_back(q, kt, vt, p, mixed_grad, span, g, head):
    lanes = slice(g * 2 * DH, (g + 1) * 2 * DH)
    kk = spread(kt)
    vv = spread(vt)
    queries = q[:, lanes]
    grad = mixed_grad[:, lanes]
    prob_grad = dot(grad, vv)
    probs = p[g]
    parts = []
    for h in range(2):
        one = probs[:, h * span : (h + 1) * span].astype(F32)
        change = prob_grad[:, h * span : (h + 1) * span]
        score = one * (change - jnp.sum(one * change, axis=1, keepdims=True))
        if head is not None:
            head(2 * g + h, score)
        parts.append(score.astype(BF16))
    score = jnp.concatenate(parts, axis=1)
    query_grad = (dot(score, kk, 1, 1) * 0.125).astype(BF16)
    key_grad = dot(queries, score, 0, 0)
    value_grad = dot(grad, probs, 0, 0)
    key_grad = key_grad[:DH, :span] + key_grad[DH:, span:]
    value_grad = value_grad[:DH, :span] + value_grad[DH:, span:]
    return query_grad, key_grad, value_grad


def cross_back(q, pair, p, mixed_grad, q_out, pair_out):
    kv = pair.shape[0] // 2
    span = pair.shape[1]
    for g in range(kv // DH):
        mine = slice(g * DH, (g + 1) * DH)
        far = slice(kv + g * DH, kv + (g + 1) * DH)
        query_grad, key_grad, value_grad = attention_back(
            q, pair[mine], pair[far], p, mixed_grad, span, g, None
        )
        q_out[:, g * 2 * DH : (g + 1) * 2 * DH] = query_grad
        pair_out[mine] = key_grad.astype(BF16)
        pair_out[far] = value_grad.astype(BF16)


def cross_grads(branch, mixed, normed, q_grad, middle, grad, gain, w0, w1, w2, w3, s0, s1, s2, s3,
                grad_out, gain_out, branch_out, mixed_out, g0, g1, g2, g3):
    width = middle.shape[1]
    size = width // 4
    dq = q_grad[...]
    for p, g in enumerate((g0, g1, g2, g3)):
        g[:, :width] = dot(rows_of(normed, p), dq, 0, 0).astype(BF16)
        g[:, width:] = dot(rows_of(branch, p), mixed[...], 0, 0).astype(BF16)
    dn = project_back(dq, [w[...] for w in (w0, w1, w2, w3)])
    back, gain_grad = norm_back(middle[...], gain[...], dn)
    total = grad[...] + back
    grad_out[...] = total
    gain_out[...] = gain_grad
    low = total.astype(BF16)
    branch_out[...] = low
    mixed_out[...] = project(low, [s[...] for s in (s0, s1, s2, s3)]).astype(BF16)


def self_back(q, kt, vt, p, mixed_grad, out, diagonal_out):
    length = q.shape[0]
    width = q.shape[1]
    kv = kt.shape[0]

    def head(h, score):
        diagonal_out[h] = diagonals(score)

    keys = []
    values = []
    for g in range(kv // DH):
        mine = slice(g * DH, (g + 1) * DH)
        query_grad, key_grad, value_grad = attention_back(
            q, kt[mine], vt[mine], p, mixed_grad, length, g, head
        )
        out[:, g * 2 * DH : (g + 1) * 2 * DH] = query_grad
        keys.append(key_grad)
        values.append(value_grad)
    out[:, width:] = jnp.concatenate(keys + values, axis=0).T.astype(BF16)


def self_grads(normed_t, grads, g0, g1, g2, g3):
    size = normed_t.shape[0] // 4
    for p, g in enumerate((g0, g1, g2, g3)):
        g[...] = dot(normed_t[p * size : (p + 1) * size], grads[...]).astype(BF16)


def restore(value, order):
    high = value.astype(BF16)
    low = (value - high.astype(F32)).astype(BF16)
    return dot(high, order, 1, 1) + dot(low, order, 1, 1)


def self_end(x, grad, grads, gain, order, w0, w1, w2, w3, input_out, gain_out):
    dn = project_back(grads[...], [w[...] for w in (w0, w1, w2, w3)])
    back, gain_grad = norm_back(x[...].astype(F32), gain[...], dn)
    input_out[...] = restore(grad[...] + back, order[...])
    gain_out[...] = gain_grad


def memory_grads(memory_t, pair_t, branch, mixed, g0, g1, g2, g3):
    size = memory_t.shape[0] // 4
    width = pair_t.shape[0]
    pair = transposed(pair_t[...])
    for p, g in enumerate((g0, g1, g2, g3)):
        g[:, :width] = dot(memory_t[p * size : (p + 1) * size], pair).astype(BF16)
        g[:, width:] = dot(rows_of(branch, p), mixed[...], 0, 0).astype(BF16)


def memory_end(pair_t, order, w0, w1, w2, w3, out):
    pair = transposed(pair_t[...])
    out[...] = restore(project_back(pair, [w[...] for w in (w0, w1, w2, w3)]), order[...])


def shape(dims, kind):
    return jax.ShapeDtypeStruct(dims, kind)


def full(value):
    return pl.BlockSpec(value.shape, lambda i, rank=len(value.shape): (0,) * rank)


def columns(value, size, place):
    return pl.BlockSpec((value.shape[0], size), lambda i, place=place: (0, place))


def call(body, outs, args, specs=None, flops=0):
    specs = [full(a) if s is None else s for a, s in zip(args, specs or [None] * len(args))]
    moved = sum(int(np.prod(o.shape)) * o.dtype.itemsize for o in outs)
    moved += sum(int(np.prod(s.block_shape)) * a.dtype.itemsize for a, s in zip(args, specs))
    return pl.pallas_call(
        body,
        grid=(1,),
        in_specs=specs,
        out_specs=[full(o) for o in outs],
        out_shape=outs,
        compiler_params=pltpu.CompilerParams(vmem_limit_bytes=VMEM),
        cost_estimate=pl.CostEstimate(flops=flops, bytes_accessed=moved, transcendentals=0),
    )(*args)


def ffn(n, nt, dy, dyt, res, dn, pieces):
    tiles = pieces[0].shape[1] // (3 * TILE)
    piece = pl.BlockSpec((pieces[0].shape[0], 3 * TILE), lambda j: (0, j))
    keep = lambda v: pl.BlockSpec(v.shape, lambda j: (0, 0))
    outs = [shape(res.shape, F32), shape(dn.shape, F32)] + [shape(w.shape, BF16) for w in pieces]
    work = n.shape[0] * n.shape[1] * TILE * 3 * 3 * 2 * tiles
    return pl.pallas_call(
        ffn_tile,
        grid=(tiles,),
        in_specs=[keep(n), keep(nt), keep(dy), keep(dyt), keep(res), keep(dn)] + [piece] * 4,
        out_specs=[keep(res), keep(dn)] + [piece] * 4,
        out_shape=outs,
        compiler_params=pltpu.CompilerParams(vmem_limit_bytes=VMEM),
        cost_estimate=pl.CostEstimate(
            flops=work, bytes_accessed=16 * pieces[0].size + 16 * res.size, transcendentals=0
        ),
    )(n, nt, dy, dyt, res, dn, *pieces)


def shards(
    nm,
    nd,
    block_input,
    memory,
    out_grad,
    decoder_segments,
    encoder_segments,
    distance_buckets,
    self_gain,
    cross_gain,
    ffn_gain,
    position_bias,
    self_query,
    self_key,
    self_value,
    self_out,
    cross_query,
    cross_key,
    cross_value,
    cross_out,
    ffn_gate,
    ffn_up,
    ffn_down,
):
    n = nm * nd
    length, width = block_input.shape[2:]
    span = encoder_segments.shape[2]
    keys = self_key.shape[1]
    rows = self_query.shape[0]
    heads = position_bias.shape[1]
    buckets = position_bias.shape[0]
    hidden = ffn_gate.shape[1]
    place = lax.axis_index("mem")
    me = place * nd + lax.axis_index("dp")

    tiles = hidden // TILE
    first = (tiles + 1) // 2
    split = lambda w: w.reshape(rows, tiles, 1, TILE)
    ffn_shard = jnp.concatenate([split(ffn_gate), split(ffn_up), split(ffn_down)], axis=2)
    ffn_shard = ffn_shard.reshape(rows, 3 * hidden)
    cut = first * 3 * TILE
    self_w = gather(jnp.concatenate([self_query, self_key, self_value, self_out], axis=1), n)
    cross_w = gather(jnp.concatenate([cross_query, cross_out, cross_key, cross_value], axis=1), n)
    ffn_a = gather(ffn_shard[:, :cut], n)
    ffn_b = gather(ffn_shard[:, cut:], n)

    src = source(n, me)
    feature = (src[:, None] * rows + lax.iota(jnp.int32, rows)[None, :]).reshape(width)
    order = (lax.iota(jnp.int32, width)[:, None] == feature[None, :]).astype(BF16)
    small = (lax.iota(jnp.int32, n)[:, None] == src[None, :]).astype(F32)

    def reorder(value):
        return jnp.dot(value, order, preferred_element_type=F32).astype(BF16)

    def reorder_gain(gain):
        return jnp.dot(small.T, gain.reshape(n, rows), precision=HIGHEST).reshape(1, width)

    x = reorder(block_input.reshape(length, width))
    dy = reorder(out_grad.reshape(length, width))
    dyt = dy.T
    gains = [reorder_gain(g) for g in (self_gain, cross_gain, ffn_gain)]
    wide = x.astype(F32)
    scale = lax.rsqrt(jnp.mean(wide * wide, axis=1, keepdims=True) + EPSILON)
    self_normed = (wide * scale * gains[0]).astype(BF16)
    self_normed_t = self_normed.T
    local = memory.reshape(nm, span // nm, width)
    local = jnp.concatenate(
        [lax.dynamic_index_in_dim(local, place ^ t, 0, keepdims=False) for t in range(nm)], axis=0
    )
    local = reorder(local)
    local_t = local.T
    seg_col = decoder_segments.reshape(length, 1)
    seg_row = decoder_segments.reshape(1, length)
    key_seg = encoder_segments.reshape(nm, span // nm)
    key_seg = jnp.concatenate(
        [lax.dynamic_index_in_dim(key_seg, place ^ t, 0, keepdims=True) for t in range(nm)], axis=1
    )
    one_hot = (distance_buckets[:, None] == lax.iota(jnp.int32, buckets)[None, :]).astype(F32)
    distance_bias = jnp.dot(one_hot, position_bias, precision=HIGHEST).T
    line = jnp.roll(distance_bias[:, ::-1], 1, axis=1)
    start = jnp.stack([jnp.roll(line, i, axis=1) for i in range(8)], axis=1)

    stream = (length, width)
    kv = keys
    groups = kv // DH
    q, kt, vt, p, mixed, middle, cross_normed = call(
        self_forward,
        [
            shape(stream, BF16),
            shape((kv, length), BF16),
            shape((kv, length), BF16),
            shape((groups, length, 2 * length), BF16),
            shape(stream, BF16),
            shape(stream, F32),
            shape(stream, BF16),
        ],
        (x, self_normed, start, seg_col, seg_row, gains[1], *self_w),
        flops=2 * length * width * 3 * width,
    )
    pair_spec = [columns(w, 2 * kv, 2 * width // (2 * kv)) for w in cross_w]
    (pair_t,) = call(
        memory_forward,
        [shape((2 * kv, span), BF16)],
        (local, *cross_w),
        [None] + pair_spec,
        flops=2 * span * width * 2 * kv,
    )
    part = span // nm
    pair_t = jnp.concatenate(
        swap_rows([pair_t[:, t * part : (t + 1) * part] for t in range(nm)], nm, nd), axis=1
    )
    cross_q, cross_p, cross_mixed, second, ffn_normed, ffn_normed_t = call(
        cross_forward,
        [
            shape(stream, BF16),
            shape((groups, length, 2 * span), BF16),
            shape(stream, BF16),
            shape(stream, F32),
            shape(stream, BF16),
            shape((width, length), BF16),
        ],
        (middle, cross_normed, pair_t, seg_col, key_seg, gains[2], *cross_w),
        [None] * 6 + [columns(w, 2 * width, 0) for w in cross_w],
        flops=2 * length * width * 2 * width,
    )

    zero = jnp.zeros(stream, F32)
    res, dn, *grads_a = ffn(ffn_normed, ffn_normed_t, dy, dyt, zero, zero, ffn_a)
    res, dn, *grads_b = ffn(ffn_normed, ffn_normed_t, dy, dyt, res, dn, ffn_b)
    done_a = scatter(grads_a, n)
    done_b = scatter(grads_b, n)

    result, grad, ffn_gain_grad, branch, mixed_grad = call(
        ffn_end,
        [
            shape(stream, BF16),
            shape(stream, F32),
            shape((1, width), F32),
            shape(stream, BF16),
            shape(stream, BF16),
        ],
        (second, res, dn, dy, gains[2], *cross_w),
        [None] * 5 + [columns(w, width, 1) for w in cross_w],
        flops=2 * length * width * width,
    )
    cross_q_grad, pair_grad_t = call(
        cross_back,
        [shape(stream, BF16), shape((2 * kv, span), BF16)],
        (cross_q, pair_t, cross_p, mixed_grad),
        flops=2 * length * span * width * 8,
    )
    pair_grad_t = jnp.concatenate(
        swap_rows([pair_grad_t[:, t * part : (t + 1) * part] for t in range(nm)], nm, nd), axis=1
    )
    pieces = [shape((width // 4, 2 * width), BF16)] * 4
    grad, cross_gain_grad, branch, mixed_grad, *grads_c = call(
        cross_grads,
        [shape(stream, F32), shape((1, width), F32), shape(stream, BF16), shape(stream, BF16)] + pieces,
        (branch, cross_mixed, cross_normed, cross_q_grad, middle, grad, gains[1], *cross_w, *self_w),
        [None] * 7 + [columns(w, width, 0) for w in cross_w] + [columns(w, width, 2) for w in self_w],
        flops=2 * length * width * width * 4,
    )
    done_c = scatter(grads_c, n)
    grads_m = call(
        memory_grads,
        [shape((width // 4, 2 * kv + width), BF16)] * 4,
        (local_t, pair_grad_t, branch, mixed),
        flops=2 * (span + length) * width * width,
    )
    done_m = scatter(grads_m, n)
    grads, diagonal = call(
        self_back,
        [shape((length, width + 2 * kv), BF16), shape((heads, 8, length), F32)],
        (q, kt, vt, p, mixed_grad),
        flops=2 * length * length * width * 8,
    )
    grads_s = call(
        self_grads,
        [shape((width // 4, width + 2 * kv), BF16)] * 4,
        (self_normed_t, grads),
        flops=2 * length * width * 2 * width,
    )
    done_s = scatter(grads_s, n)
    input_grad, self_gain_grad = call(
        self_end,
        [shape(stream, F32), shape((1, width), F32)],
        (x, grad, grads, gains[0], order, *self_w),
        [None] * 5 + [columns(w, width + 2 * kv, 0) for w in self_w],
        flops=2 * length * width * 4 * width,
    )
    (memory_grad,) = call(
        memory_end,
        [shape((span, width), F32)],
        (pair_grad_t, order, *cross_w),
        [None] * 2 + pair_spec,
        flops=2 * span * width * 3 * width,
    )
    memory_grad = memory_grad.reshape(nm, part, width)
    memory_grad = jnp.stack(
        [lax.dynamic_index_in_dim(memory_grad, place ^ t, 0, keepdims=False) for t in range(nm)]
    )
    result = lax.dot_general(
        result, order, (((1,), (1,)), ((), ())), preferred_element_type=F32
    ).astype(BF16)

    by_row = sum(jnp.roll(diagonal[:, i], -i, axis=1) for i in range(8))
    by_distance = jnp.roll(by_row, -1, axis=1)[:, ::-1]
    table = jnp.dot(by_distance, one_hot, precision=HIGHEST).T
    gain_grads = jnp.concatenate([self_gain_grad, cross_gain_grad, ffn_gain_grad], axis=0)
    gain_grads = jnp.einsum("sd,gdr->gsr", small, gain_grads.reshape(3, n, rows), precision=HIGHEST)
    packed = jnp.concatenate([gain_grads.reshape(-1, 128), table.reshape(-1, 128)], axis=0)
    packed = sum_all(packed, n)
    gain_grads = packed[: 3 * width // 128].reshape(3, width)
    table = packed[3 * width // 128 :].reshape(buckets, heads)

    ffn_done = jnp.concatenate([done_a, done_b], axis=1).reshape(rows, tiles, 3, TILE)
    return (
        result.reshape(block_input.shape),
        input_grad.reshape(block_input.shape),
        memory_grad.reshape(memory.shape),
        gain_grads[0],
        gain_grads[1],
        gain_grads[2],
        table,
        done_s[:, :width],
        done_s[:, width : width + kv],
        done_s[:, width + kv :],
        done_m[:, 2 * kv :],
        done_c[:, :width],
        done_m[:, :kv],
        done_m[:, kv : 2 * kv],
        done_c[:, width:],
        ffn_done[:, :, 0].reshape(rows, hidden),
        ffn_done[:, :, 1].reshape(rows, hidden),
        ffn_done[:, :, 2].reshape(rows, hidden),
    )


def solution(mesh):
    stream = P("dp", "mem", None, None)
    segments = P("dp", "mem", None)
    shard = P(AXES, None)
    in_specs = (stream, P("dp", None, "mem", None), stream, segments, segments) + (P(),) * 5 + (shard,) * 11
    out_specs = (stream, stream, P("dp", None, "mem", None)) + (P(),) * 4 + (shard,) * 11
    body = functools.partial(shards, mesh.shape["mem"], mesh.shape["dp"])
    return jax.shard_map(body, mesh=mesh, in_specs=in_specs, out_specs=out_specs, check_vma=False)
```

time: 2300 us -> 554 us (0.24)
  waiting for transfers between devices: 1910 us -> 294 us
  matrix products: 138 us -> 8.4 us
  Pallas kernels: 0 us -> 106 us
  local copies, waits for them, and re-layouts: 121 us -> 46.7 us
  blocking collectives: 70.8 us -> 0 us
  starting transfers between devices: 4.4 us -> 52.3 us
    reduce_scatter x8 -> x0, waiting for transfers between devices: 914 us -> none  [the longest x2 279 us: reduce_attention(): lax.psum_scatter(first, ('mem', 'dp'), scatter_dimension=0, tiled=True)]
    all_gather x11 -> x0, waiting for transfers between devices: 570 us -> none  [the longest x2 108 us: fetch_attention(): lax.all_gather(third, ('mem', 'dp'), axis=0, tiled=True)]
    unnamed x25 -> x0, waiting for transfers between devices: 431 us -> none
    ppermute x0 -> x65, waiting for transfers between devices: none -> 294 us  [the longest x15 114 us: scatter(): came = lax.ppermute(held[half:].astype(BF16), AXES, exchange(n, k))]
    dot_general x43 -> x9, matrix products: 137 us -> 8.2 us  [the longest x3 4.19 us: reorder(): return jnp.dot(value, order, preferred_element_type=F32).astype(BF16)]
    pallas_call x0 -> x13, Pallas kernels: none -> 106 us  [the longest x11 79.1 us: call(): pl.pallas_call(body, grid=(1,), in_specs=specs, out_specs=[full(o) for o...]
    ppermute x0 -> x65, starting transfers between devices: none -> 52.3 us  [the longest x12 13.3 us: gather(): lax.ppermute(held, AXES, exchange(n, k))]
    psum x1 -> x0, blocking collectives: 38.6 us -> none  [shards(): lax.psum((self_gain_grad, cross_gain_grad, ffn_gain_grad, table_grad), ('...]
  transfers between devices with their start and end apart: 23 -> 65, of which waited for: 21 -> 35; matrix products, arithmetic and copies ran while one was open for 10% -> 14% of each run, Pallas kernels for 0% -> 10%
where the time goes in v1:
time: 554 us; the launch traced here: 548 us
  waiting for transfers between devices  294 us (53%)
  Pallas kernels  106 us (19%)
  starting transfers between devices  52.3 us (9%)
  local copies, waits for them, and re-layouts  46.7 us (8%)
  other arithmetic  37.9 us (7%)
  matrix products  8.4 us (2%)
    ppermute x15, waiting for transfers between devices, scatter(): came = lax.ppermute(held[half:].astype(BF16), AXES, exchange(n, k))  114 us
    ppermute x12, waiting for transfers between devices, gather(): lax.ppermute(held, AXES, exchange(n, k))  94.4 us
    pallas_call x11, Pallas kernels, call(): pl.pallas_call(body, grid=(1,), in_specs=specs, out_specs=[full(o) for o...  79.1 us
    ppermute x4, waiting for transfers between devices, gather(): pieces = [held, lax.ppermute(held, AXES, exchange(n, last))]  28.9 us
    ppermute x5, waiting for transfers between devices, scatter(): held = held + lax.ppermute(send, AXES, exchange(n, last)).astype(F32)  27.4 us
    pallas_call x2, Pallas kernels, ffn(): pl.pallas_call(ffn_tile, grid=(tiles,), in_specs=[keep(n), keep(nt), keep...  27.4 us
    ppermute x5, waiting for transfers between devices, sum_all(): lax.ppermute(value, AXES, [(d, d ^ 1 << bit) for d in range(n)])  15.1 us
    concatenate x12, other arithmetic, gather(): jnp.concatenate([held, lax.ppermute(held, AXES, exchange(n, k))], axis=0)  14.9 us
  transfers between devices with their start and end apart: 65, of which 35 were waited for; matrix products, arithmetic and copies ran while one was open for 14% of the time, Pallas kernels for 10%

profile of v1, /device:TPU:0, one launch (start us, length us, event | category | flops | bytes accessed | tf_op | source)
XLA Modules:
  0.0 547.6 jit_solution(13719474482784454650)
XLA Ops:
  3.9 4.0 collective-permute-start.6
  15.8 2.9 collective-permute-start.15
  20.7 2.2 dynamic-slice_bitcast_fusion.3
  23.4 10.5 %collective-permute-done.6 = bf16[32,3072]{1,0:T(8,128)(2,1)} collective-permute-done((bf16[32,3072]{1,0:T(8,128)(2,1)S(1)}, bf16[32,3072]{1,0:T(8,128)(2,1)}, u32[]{:S(2)}, u32[]{:S(2)}) %collective-permute-start.6) | collective-permute-done | bytes 196640 | tf_op jit(solution)/shard_map/ppermute | solution.py:55
  34.9 3.3 collective-permute-done
  39.2 5.2 collective-permute-done.15
  44.5 4.3 collective-permute-done.21
  49.6 7.7 %collective-permute-done.7 = bf16[64,3072]{1,0:T(8,128)(2,1)S(1)} collective-permute-done((bf16[64,3072]{1,0:T(8,128)(2,1)S(1)}, bf16[64,3072]{1,0:T(8,128)(2,1)S(1)}, u32[]{:S(2)}, u32[]{:S(2)}) %collective-permute-start.7) | collective-permute-done | bytes 393248 | tf_op jit(solution)/shard_map/ppermute | solution.py:55
  59.8 18.4 %collective-permute-done.16 = bf16[64,4608]{1,0:T(8,128)(2,1)S(1)} collective-permute-done((bf16[64,4608]{1,0:T(8,128)(2,1)S(1)}, bf16[64,4608]{1,0:T(8,128)(2,1)S(1)}, u32[]{:S(2)}, u32[]{:S(2)}) %collective-permute-start.16) | collective-permute-done | bytes 589856 | tf_op jit(solution)/shard_map/ppermute | solution.py:55
  80.0 2.0 pad_maximum_fusion.9
  85.1 3.7 collective-permute-done.22
  88.8 2.0 pad_maximum_fusion.8
  92.4 11.2 %collective-permute-done.17 = bf16[128,4608]{1,0:T(8,128)(2,1)S(1)} collective-permute-done((bf16[128,4608]{1,0:T(8,128)(2,1)S(1)}, bf16[128,4608]{1,0:T(8,128)(2,1)S(1)}, u32[]{:S(2)}, u32[]{:S(2)}) %collective-permute-start.17) | collective-permute-done | bytes 1179680 | tf_op jit(solution)/shard_map/ppermute | solution.py:55
  107.0 13.6 %collective-permute-done.2 = bf16[128,3072]{1,0:T(8,128)(2,1)} collective-permute-done((bf16[128,3072]{1,0:T(8,128)(2,1)}, bf16[128,3072]{1,0:T(8,128)(2,1)}, u32[]{:S(2)}, u32[]{:S(2)}) %collective-permute-start.2) | collective-permute-done | bytes 786464 | tf_op jit(solution)/shard_map/ppermute | solution.py:55
  120.6 2.6 pad_maximum_fusion.2.w0.s0
  125.2 16.5 %collective-permute-done.23 = bf16[128,3840]{1,0:T(8,128)(2,1)} collective-permute-done((bf16[128,3840]{1,0:T(8,128)(2,1)}, bf16[128,3840]{1,0:T(8,128)(2,1)}, u32[]{:S(2)}, u32[]{:S(2)}) %collective-permute-start.23) | collective-permute-done | bytes 983072 | tf_op jit(solution)/shard_map/ppermute | solution.py:55
  141.7 2.7 pad_maximum_fusion.1.w0
  146.3 2.5 fusion.7
  149.1 22.5 %collective-permute-done.3.w1.s1 = bf16[256,3072]{1,0:T(8,128)(2,1)} collective-permute-done((bf16[256,3072]{1,0:T(8,128)(2,1)}, bf16[256,3072]{1,0:T(8,128)(2,1)}, u32[]{:S(2)}, u32[]{:S(2)}) %collective-permute-start.3) | collective-permute-done | bytes 1572896 | tf_op jit(solution)/shard_map/ppermute | solution.py:56
  182.0 4.1 shard_map.377
  186.3 6.4 %collective-permute-done.24.w1 = bf16[256,3840]{1,0:T(8,128)(2,1)} collective-permute-done((bf16[256,3840]{1,0:T(8,128)(2,1)}, bf16[256,3840]{1,0:T(8,128)(2,1)}, u32[]{:S(2)}, u32[]{:S(2)}) %collective-permute-start.24) | collective-permute-done | bytes 1966112 | tf_op jit(solution)/shard_map/ppermute | solution.py:56
  193.6 2.1 fusion.57
  199.3 4.8 collective-permute-done.12
  204.1 2.4 collective-permute-start.13
  206.4 2.3 fusion.3.order
  208.7 9.5 %collective-permute-done.13 = bf16[1024,128]{1,0:T(8,128)(2,1)S(1)} collective-permute-done((bf16[1024,128]{1,0:T(8,128)(2,1)}, bf16[1024,128]{1,0:T(8,128)(2,1)S(1)}, u32[]{:S(2)}, u32[]{:S(2)}) %collective-permute-start.13) | collective-permute-done | bytes 262176 | tf_op jit(solution)/shard_map/ppermute | solution.py:82
  218.2 3.5 collective-permute-start.14
  222.3 9.9 %shard_map.376 = (bf16[256,1024]{1,0:T(8,128)(2,1)}, bf16[512,256]{1,0:T(8,128)(2,1)}, bf16[512,256]{1,0:T(8,128)(2,1)}, bf16[8,256,512]{2,1,0:T(8,128)(2,1)}, b...) custom-call(bf16[256,1024]{1,0:T(8,128)(2,1)} %copy.76.x, ...), custom_call_target="tpu_custom_call" | custom-call | flops 1610612736 | bytes 12720128 | tf_op jit(solution)/shard_map/pallas_call | solution.py:377
  233.3 11.0 %shard_map.378 = (bf16[256,1024]{1,0:T(8,128)(2,1)}, bf16[8,256,1024]{2,1,0:T(8,128)(2,1)}, bf16[256,1024]{1,0:T(8,128)(2,1)}, f32[256,1024]{1,0:T(8,128)}, bf16...) custom-call(f32[256,1024]{1,0:T(8,128)} %get-tuple-element.70.middle, bf16[256,1024]{1,0:T(8,128)(2,1)} %get-tuple-element.71.normed, ...), custom_call_target="tpu_custom_call" | custom-call | flops 1073741824 | bytes 14162944 | tf_op jit(solution)/shard_map/pallas_call | solution.py:377
  245.4 14.4 %shard_map.379 = (f32[256,1024]{1,0:T(8,128)}, f32[256,1024]{1,0:T(8,128)}, bf16[256,4608]{1,0:T(8,128)(2,1)}, bf16[256,4608]{1,0:T(8,128)(2,1)}, bf16[256,4608]{1,0:T(8,128)(2,1)}, /*index=5*/bf16[256,4608]{1,0:T(8,128)(2,1)}) custom-call(bf16[256,1024]{1,0:T(8,128)(2,1)} %get-tuple-element.73.n, bf16[1024,256]{1,0:T(8,128)(2,1)} %get-tuple-element.74.nt, ...), custom_call_target="tpu_custom_call" | custom-call | flops 7247757312 | bytes 23068672 | tf_op jit(solution)/shard_map/pallas_call | solution.py:394
  259.9 12.9 %shard_map.380 = (f32[256,1024]{1,0:T(8,128)}, f32[256,1024]{1,0:T(8,128)}, bf16[256,3840]{1,0:T(8,128)(2,1)}, bf16[256,3840]{1,0:T(8,128)(2,1)}, bf16[256,3840]{1,0:T(8,128)(2,1)}, /*index=5*/bf16[256,3840]{1,0:T(8,128)(2,1)}) custom-call(bf16[256,1024]{1,0:T(8,128)(2,1)} %get-tuple-element.73.n, bf16[1024,256]{1,0:T(8,128)(2,1)} %get-tuple-element.74.nt, ...), custom_call_target="tpu_custom_call" | custom-call | flops 6039797760 | bytes 19922944 | tf_op jit(solution)/shard_map/pallas_call | solution.py:394
  272.8 4.8 shard_map.381
  277.6 8.8 %shard_map.382 = (bf16[256,1024]{1,0:T(8,128)(2,1)}, bf16[1024,512]{1,0:T(8,128)(2,1)}) custom-call(bf16[256,1024]{1,0:T(8,128)(2,1)} %get-tuple-element.82.q, bf16[1024,512]{1,0:T(8,128)(2,1)} %pad_maximum_fusion.6.pair, bf16[8,256,1024]{2,1,0:T(8,128)(2,1)} %get-tuple-element.83.p, bf16[256,1024]{1,0:T(8,128)(2,1)} %get-tuple-element.84.mixed_grad), custom_call_target="tpu_custom_call" | custom-call | flops 2147483648 | bytes 7864320 | tf_op jit(solution)/shard_map/pallas_call | solution.py:377
  286.4 7.7 %shard_map.383 = (f32[256,1024]{1,0:T(8,128)}, f32[1,1024]{1,0:T(1,128)}, bf16[256,1024]{1,0:T(8,128)(2,1)}, bf16[256,1024]{1,0:T(8,128)(2,1)}, bf16[256,2048]{1...) custom-call(bf16[256,1024]{1,0:T(8,128)(2,1)} %get-tuple-element.80.branch, ...), custom_call_target="tpu_custom_call" | custom-call | flops 2147483648 | bytes 14688256 | tf_op jit(solution)/shard_map/pallas_call | solution.py:377
  294.1 9.4 %shard_map.384 = (bf16[256,2048]{1,0:T(8,128)(2,1)}, f32[16,8,256]{2,1,0:T(8,128)}) custom-call(bf16[256,1024]{1,0:T(8,128)(2,1)} %get-tuple-element.88.q, bf16[512,256]{1,0:T(8,128)(2,1)} %get-tuple-element.89.kt, bf16[512,256]{1,0:T(8,128)(2,1)} %get-tuple-element.90.vt, bf16[8,256,512]{2,1,0:T(8,128)(2,1)} %get-tuple-element.91.p, ...), custom_call_target="tpu_custom_call" | custom-call | flops 1073741824 | bytes 4849664 | tf_op jit(solution)/shard_map/pallas_call | solution.py:377
  306.8 7.3 %shard_map.385 = (f32[256,1024]{1,0:T(8,128)}, f32[1,1024]{1,0:T(1,128)}) custom-call(bf16[256,1024]{1,0:T(8,128)(2,1)} %copy.76.x, f32[256,1024]{1,0:T(8,128)} %get-tuple-element.87.grad, bf16[256,2048]{1,0:T(8,128)(2,1)} %get-tuple-element.93.grads, f32[1,1024]{1,0:T(1,128)} %reshape.180.gain, bf16[1024,1024]{1,0:T(8,128)(2,1)} %fusion.3.order, ...), custom_call_target="tpu_custom_call" | custom-call | flops 2147483648 | bytes 9969664 | tf_op jit(solution)/shard_map/pallas_call | solution.py:377
  321.9 2.1 fusion.56
  324.8 3.5 collective-permute-start.29
  328.4 2.9 fusion.10
  331.3 9.7 %collective-permute-done.33 = f32[28,128]{1,0:T(8,128)S(1)} collective-permute-done((f32[28,128]{1,0:T(8,128)S(1)}, f32[28,128]{1,0:T(8,128)S(1)}, u32[]{:S(2)}, u32[]{:S(2)}) %collective-permute-start.33) | collective-permute-done | bytes 14368 | tf_op jit(solution)/shard_map/ppermute | solution.py:75
  341.0 2.2 collective-permute-start.34
  343.2 3.8 shard_map.387
  347.0 3.1 collective-permute-done.34
  353.3 2.3 pad_maximum_fusion.7.pair_t
  355.7 7.3 %shard_map.386 = f32[512,1024]{1,0:T(8,128)} custom-call(bf16[1024,512]{1,0:T(8,128)(2,1)} %pad_maximum_fusion.7.pair_t, bf16[1024,1024]{1,0:T(8,128)(2,1)} %fusion.3.order, bf16[256,3072]{1,0:T(8,128)(2,1)} %copy-done.2, bf16[256,3072]{1,0:T(8,128)(2,1)} %collective-permute-done.9.w1, bf16[256,3072]{1,0:T(8,128)(2,1)} %collective-permute-done.10.w2, ...), custom_call_target="tpu_custom_call" | custom-call | flops 3221225472 | bytes 7340032 | tf_op jit(solution)/shard_map/pallas_call | solution.py:377
  362.9 4.9 shard_map.388
  376.9 2.2 add_convert_fusion.1
  379.3 9.7 %collective-permute-done.49 = bf16[256,2048]{1,0:T(8,128)(2,1)S(1)} collective-permute-done((bf16[256,2048]{1,0:T(8,128)(2,1)S(1)}, bf16[256,2048]{1,0:T(8,128)(2,1)S(1)}, u32[]{:S(2)}, u32[]{:S(2)}) %collective-permute-start.49) | collective-permute-done | bytes 1048608 | tf_op jit(solution)/shard_map/ppermute | solution.py:65
  391.9 8.4 %collective-permute-done.37 = bf16[256,2048]{1,0:T(8,128)(2,1)S(1)} collective-permute-done((bf16[256,2048]{1,0:T(8,128)(2,1)S(1)}, bf16[256,2048]{1,0:T(8,128)(2,1)S(1)}, u32[]{:S(2)}, u32[]{:S(2)}) %collective-permute-start.37) | collective-permute-done | bytes 1048608 | tf_op jit(solution)/shard_map/ppermute | solution.py:65
  402.1 9.3 %collective-permute-done.43 = bf16[256,2048]{1,0:T(8,128)(2,1)S(1)} collective-permute-done((bf16[256,2048]{1,0:T(8,128)(2,1)S(1)}, bf16[256,2048]{1,0:T(8,128)(2,1)S(1)}, u32[]{:S(2)}, u32[]{:S(2)}) %collective-permute-start.43) | collective-permute-done | bytes 1048608 | tf_op jit(solution)/shard_map/ppermute | solution.py:65
  414.7 11.6 %collective-permute-done.50 = bf16[128,2048]{1,0:T(8,128)(2,1)S(1)} collective-permute-done((bf16[128,2048]{1,0:T(8,128)(2,1)S(1)}, bf16[128,2048]{1,0:T(8,128)(2,1)S(1)}, u32[]{:S(2)}, u32[]{:S(2)}) %collective-permute-start.50) | collective-permute-done | bytes 524320 | tf_op jit(solution)/shard_map/ppermute | solution.py:68
  427.0 10.5 %collective-permute-done.38 = bf16[128,2048]{1,0:T(8,128)(2,1)S(1)} collective-permute-done((bf16[128,2048]{1,0:T(8,128)(2,1)S(1)}, bf16[128,2048]{1,0:T(8,128)(2,1)S(1)}, u32[]{:S(2)}, u32[]{:S(2)}) %collective-permute-start.38) | collective-permute-done | bytes 524320 | tf_op jit(solution)/shard_map/ppermute | solution.py:68
  437.8 6.4 %collective-permute-done.51 = bf16[64,2048]{1,0:T(8,128)(2,1)S(1)} collective-permute-done((bf16[64,2048]{1,0:T(8,128)(2,1)S(1)}, bf16[64,2048]{1,0:T(8,128)(2,1)S(1)}, u32[]{:S(2)}, u32[]{:S(2)}) %collective-permute-start.51) | collective-permute-done | bytes 262176 | tf_op jit(solution)/shard_map/ppermute | solution.py:68
  445.4 3.4 collective-permute-done.44
  448.9 6.5 %collective-permute-done.39 = bf16[64,2048]{1,0:T(8,128)(2,1)S(1)} collective-permute-done((bf16[64,2048]{1,0:T(8,128)(2,1)S(1)}, bf16[64,2048]{1,0:T(8,128)(2,1)S(1)}, u32[]{:S(2)}, u32[]{:S(2)}) %collective-permute-start.39) | collective-permute-done | bytes 262176 | tf_op jit(solution)/shard_map/ppermute | solution.py:68
  455.5 9.5 %collective-permute-done.52 = bf16[32,2048]{1,0:T(8,128)(2,1)S(1)} collective-permute-done((bf16[32,2048]{1,0:T(8,128)(2,1)S(1)}, bf16[32,2048]{1,0:T(8,128)(2,1)S(1)}, u32[]{:S(2)}, u32[]{:S(2)}) %collective-permute-start.52) | collective-permute-done | bytes 131104 | tf_op jit(solution)/shard_map/ppermute | solution.py:68
  465.1 5.9 %collective-permute-done.40 = bf16[32,2048]{1,0:T(8,128)(2,1)S(1)} collective-permute-done((bf16[32,2048]{1,0:T(8,128)(2,1)S(1)}, bf16[32,2048]{1,0:T(8,128)(2,1)S(1)}, u32[]{:S(2)}, u32[]{:S(2)}) %collective-permute-start.40) | collective-permute-done | bytes 131104 | tf_op jit(solution)/shard_map/ppermute | solution.py:68
  472.4 6.4 %collective-permute-done.45 = bf16[64,2048]{1,0:T(8,128)(2,1)S(1)} collective-permute-done((bf16[64,2048]{1,0:T(8,128)(2,1)S(1)}, bf16[64,2048]{1,0:T(8,128)(2,1)S(1)}, u32[]{:S(2)}, u32[]{:S(2)}) %collective-permute-start.45) | collective-permute-done | bytes 262176 | tf_op jit(solution)/shard_map/ppermute | solution.py:68
  480.8 4.8 collective-permute-done.46
  491.1 10.4 %collective-permute-done.62 = bf16[128,3840]{1,0:T(8,128)(2,1)S(1)} collective-permute-done((bf16[128,3840]{1,0:T(8,128)(2,1)S(1)}, bf16[128,3840]{1,0:T(8,128)(2,1)S(1)}, u32[]{:S(2)}, u32[]{:S(2)}) %collective-permute-start.62) | collective-permute-done | bytes 983072 | tf_op jit(solution)/shard_map/ppermute | solution.py:68
  501.8 12.3 %collective-permute-done.56 = bf16[128,4608]{1,0:T(8,128)(2,1)S(1)} collective-permute-done((bf16[128,4608]{1,0:T(8,128)(2,1)S(1)}, bf16[128,4608]{1,0:T(8,128)(2,1)S(1)}, u32[]{:S(2)}, u32[]{:S(2)}) %collective-permute-start.56) | collective-permute-done | bytes 1179680 | tf_op jit(solution)/shard_map/ppermute | solution.py:68
  515.1 13.5 %collective-permute-done.57 = bf16[64,4608]{1,0:T(8,128)(2,1)S(1)} collective-permute-done((bf16[64,4608]{1,0:T(8,128)(2,1)S(1)}, bf16[64,4608]{1,0:T(8,128)(2,1)S(1)}, u32[]{:S(2)}, u32[]{:S(2)}) %collective-permute-start.57) | collective-permute-done | bytes 589856 | tf_op jit(solution)/shard_map/ppermute | solution.py:68
  528.9 12.1 %collective-permute-done.58 = bf16[32,4608]{1,0:T(8,128)(2,1)S(1)} collective-permute-done((bf16[32,4608]{1,0:T(8,128)(2,1)S(1)}, bf16[32,4608]{1,0:T(8,128)(2,1)S(1)}, u32[]{:S(2)}, u32[]{:S(2)}) %collective-permute-start.58) | collective-permute-done | bytes 294944 | tf_op jit(solution)/shard_map/ppermute | solution.py:68
  541.7 2.8 slice_reduce_fusion
  (356 shorter events, 98.9 us)
Async XLA Ops:
  3.9 29.9 %collective-permute-start.6 = (bf16[32,3072]{1,0:T(8,128)(2,1)S(1)}, bf16[32,3072]{1,0:T(8,128)(2,1)}, u32[]{:S(2)}, u32[]{:S(2)}) collective-permute-start(bf16[32,3072]{1,0:T(8,128)(2,1)S(1)} %constant_dynamic-update-slice_fusion.4), channel_id=1, source_target_pairs={{0,16},{1,17},{2,18},{3,19},{4,20},{5,21},{6,22},{7,23},{8,24},{9,... | collective-permute-start | bytes 589832 | tf_op jit(solution)/shard_map/ppermute | solution.py:55
  11.2 26.9 %collective-permute-start = (bf16[32,3072]{1,0:T(8,128)(2,1)S(1)}, bf16[32,3072]{1,0:T(8,128)(2,1)}, u32[]{:S(2)}, u32[]{:S(2)}) collective-permute-start(bf16[32,3072]{1,0:T(8,128)(2,1)S(1)} %constant_dynamic-update-slice_fusion), channel_id=1, source_target_pairs={{0,16},{1,17},{2,18},{3,19},{4,20},{5,21},{6,22},{7,23},{8,24},{9,... | collective-permute-start | bytes 589832 | tf_op jit(solution)/shard_map/ppermute | solution.py:55
  15.8 28.6 %collective-permute-start.15 = (bf16[32,4608]{1,0:T(8,128)(2,1)S(1)}, bf16[32,4608]{1,0:T(8,128)(2,1)S(1)}, u32[]{:S(2)}, u32[]{:S(2)}) collective-permute-start(bf16[32,4608]{1,0:T(8,128)(2,1)S(1)} %slice.501), channel_id=1, source_target_pairs={{0,16},{1,17},{2,18},{3,19},{4,20},{5,21},{6,22},{7,23},{8,24},{9,... | collective-permute-start | bytes 884744 | tf_op jit(solution)/shard_map/ppermute | solution.py:55
  18.7 30.1 %collective-permute-start.21 = (bf16[32,3840]{1,0:T(8,128)(2,1)S(1)}, bf16[32,3840]{1,0:T(8,128)(2,1)S(1)}, u32[]{:S(2)}, u32[]{:S(2)}) collective-permute-start(bf16[32,3840]{1,0:T(8,128)(2,1)S(1)} %slice.502), channel_id=1, source_target_pairs={{0,16},{1,17},{2,18},{3,19},{4,20},{5,21},{6,22},{7,23},{8,24},{9,... | collective-permute-start | bytes 737288 | tf_op jit(solution)/shard_map/ppermute | solution.py:55
  34.8 22.4 %collective-permute-start.7 = (bf16[64,3072]{1,0:T(8,128)(2,1)S(1)}, bf16[64,3072]{1,0:T(8,128)(2,1)S(1)}, u32[]{:S(2)}, u32[]{:S(2)}) collective-permute-start(bf16[64,3072]{1,0:T(8,128)(2,1)S(1)} %pad_maximum_fusion.15), channel_id=1, source_target_pairs={{0,8},{1,9},{2,10},{3,11},{4,12},{5,13},{6,14},{7,15},{8,0},{9,1},... | collective-permute-start | bytes 1179656 | tf_op jit(solution)/shard_map/ppermute | solution.py:55
  39.1 40.9 %collective-permute-start.1 = (bf16[64,3072]{1,0:T(8,128)(2,1)S(1)}, bf16[64,3072]{1,0:T(8,128)(2,1)S(1)}, u32[]{:S(2)}, u32[]{:S(2)}) collective-permute-start(bf16[64,3072]{1,0:T(8,128)(2,1)S(1)} %pad_maximum_fusion.14), channel_id=1, source_target_pairs={{0,8},{1,9},{2,10},{3,11},{4,12},{5,13},{6,14},{7,15},{8,0},{9,1},... | collective-permute-start | bytes 1179656 | tf_op jit(solution)/shard_map/ppermute | solution.py:55
  44.4 33.9 %collective-permute-start.16 = (bf16[64,4608]{1,0:T(8,128)(2,1)S(1)}, bf16[64,4608]{1,0:T(8,128)(2,1)S(1)}, u32[]{:S(2)}, u32[]{:S(2)}) collective-permute-start(bf16[64,4608]{1,0:T(8,128)(2,1)S(1)} %pad_maximum_fusion.12), channel_id=1, source_target_pairs={{0,8},{1,9},{2,10},{3,11},{4,12},{5,13},{6,14},{7,15},{8,0},{9,1},... | collective-permute-start | bytes 1769480 | tf_op jit(solution)/shard_map/ppermute | solution.py:55
  48.8 40.0 %collective-permute-start.22 = (bf16[64,3840]{1,0:T(8,128)(2,1)S(1)}, bf16[64,3840]{1,0:T(8,128)(2,1)}, u32[]{:S(2)}, u32[]{:S(2)}) collective-permute-start(bf16[64,3840]{1,0:T(8,128)(2,1)S(1)} %pad_maximum_fusion.13), channel_id=1, source_target_pairs={{0,8},{1,9},{2,10},{3,11},{4,12},{5,13},{6,14},{7,15},{8,0},{9,1},... | collective-permute-start | bytes 1474568 | tf_op jit(solution)/shard_map/ppermute | solution.py:55
  58.2 24.3 %collective-permute-start.8 = (bf16[128,3072]{1,0:T(8,128)(2,1)S(1)}, bf16[128,3072]{1,0:T(8,128)(2,1)S(1)}, u32[]{:S(2)}, u32[]{:S(2)}) collective-permute-start(bf16[128,3072]{1,0:T(8,128)(2,1)S(1)} %pad_maximum_fusion.10), channel_id=1, source_target_pairs={{0,4},{1,3},{2,6},{3,1},{4,0},{5,7},{6,2},{7,5},{8,12},{9,11},{10,... | collective-permute-start | bytes 2359304 | tf_op jit(solution)/shard_map/ppermute | solution.py:55
  78.4 25.3 %collective-permute-start.17 = (bf16[128,4608]{1,0:T(8,128)(2,1)S(1)}, bf16[128,4608]{1,0:T(8,128)(2,1)S(1)}, u32[]{:S(2)}, u32[]{:S(2)}) collective-permute-start(bf16[128,4608]{1,0:T(8,128)(2,1)S(1)} %pad_maximum_fusion.4), channel_id=1, source_target_pairs={{0,4},{1,3},{2,6},{3,1},{4,0},{5,7},{6,2},{7,5},{8,12},{9,11},{10,... | collective-permute-start | bytes 3538952 | tf_op jit(solution)/shard_map/ppermute | solution.py:55
  82.0 38.6 %collective-permute-start.2 = (bf16[128,3072]{1,0:T(8,128)(2,1)}, bf16[128,3072]{1,0:T(8,128)(2,1)}, u32[]{:S(2)}, u32[]{:S(2)}) collective-permute-start(bf16[128,3072]{1,0:T(8,128)(2,1)} %pad_maximum_fusion.9), channel_id=1, source_target_pairs={{0,4},{1,3},{2,6},{3,1},{4,0},{5,7},{6,2},{7,5},{8,12},{9,11},{10,... | collective-permute-start | bytes 2359304 | tf_op jit(solution)/shard_map/ppermute | solution.py:55
  83.5 41.4 %collective-permute-start.9 = (bf16[256,3072]{1,0:T(8,128)(2,1)S(1)}, bf16[256,3072]{1,0:T(8,128)(2,1)}, u32[]{:S(2)}, u32[]{:S(2)}) collective-permute-start(bf16[256,3072]{1,0:T(8,128)(2,1)S(1)} %pad_maximum_fusion.3.w0), channel_id=1, source_target_pairs={{0,2},{1,5},{2,0},{3,7},{4,6},{5,1},{6,4},{7,3},{8,10},{9,13},{10,... | collective-permute-start | bytes 4718600 | tf_op jit(solution)/shard_map/ppermute | solution.py:56
  90.9 50.8 %collective-permute-start.23 = (bf16[128,3840]{1,0:T(8,128)(2,1)}, bf16[128,3840]{1,0:T(8,128)(2,1)}, u32[]{:S(2)}, u32[]{:S(2)}) collective-permute-start(bf16[128,3840]{1,0:T(8,128)(2,1)} %pad_maximum_fusion.8), channel_id=1, source_target_pairs={{0,4},{1,3},{2,6},{3,1},{4,0},{5,7},{6,2},{7,5},{8,12},{9,11},{10,... | collective-permute-start | bytes 2949128 | tf_op jit(solution)/shard_map/ppermute | solution.py:55
  105.2 71.2 %collective-permute-start.18 = (bf16[256,4608]{1,0:T(8,128)(2,1)}, bf16[256,4608]{1,0:T(8,128)(2,1)}, u32[]{:S(2)}, u32[]{:S(2)}) collective-permute-start(bf16[256,4608]{1,0:T(8,128)(2,1)} %pad_maximum_fusion.w0), channel_id=1, source_target_pairs={{0,2},{1,5},{2,0},{3,7},{4,6},{5,1},{6,4},{7,3},{8,10},{9,13},{10,... | collective-permute-start | bytes 7077896 | tf_op jit(solution)/shard_map/ppermute | solution.py:56
  107.0 41.9 %collective-permute-start.10 = (bf16[256,3072]{1,0:T(8,128)(2,1)S(1)}, bf16[256,3072]{1,0:T(8,128)(2,1)}, u32[]{:S(2)}, u32[]{:S(2)}) collective-permute-start(bf16[256,3072]{1,0:T(8,128)(2,1)S(1)} %pad_maximum_fusion.3.w0), channel_id=1, source_target_pairs={{0,1},{1,0},{2,3},{3,2},{4,5},{5,4},{6,7},{7,6},{8,9},{9,8},{10,11... | collective-permute-start | bytes 4718600 | tf_op jit(solution)/shard_map/ppermute | solution.py:57
  123.2 48.4 %collective-permute-start.3 = (bf16[256,3072]{1,0:T(8,128)(2,1)}, bf16[256,3072]{1,0:T(8,128)(2,1)}, u32[]{:S(2)}, u32[]{:S(2)}) collective-permute-start(bf16[256,3072]{1,0:T(8,128)(2,1)} %pad_maximum_fusion.2.w0.s0), channel_id=1, source_target_pairs={{0,2},{1,5},{2,0},{3,7},{4,6},{5,1},{6,4},{7,3},{8,10},{9,13},{10,... | collective-permute-start | bytes 4718600 | tf_op jit(solution)/shard_map/ppermute | solution.py:56
  124.9 51.6 %collective-permute-start.11 = (bf16[256,3072]{1,0:T(8,128)(2,1)}, bf16[256,3072]{1,0:T(8,128)(2,1)}, u32[]{:S(2)}, u32[]{:S(2)}) collective-permute-start(bf16[256,3072]{1,0:T(8,128)(2,1)} %collective-permute-done.9.w1), channel_id=1, source_target_pairs={{0,1},{1,0},{2,3},{3,2},{4,5},{5,4},{6,7},{7,6},{8,9},{9,8},{10,11... | collective-permute-start | bytes 4718600 | tf_op jit(solution)/shard_map/ppermute | solution.py:57
  144.4 48.3 %collective-permute-start.24 = (bf16[256,3840]{1,0:T(8,128)(2,1)}, bf16[256,3840]{1,0:T(8,128)(2,1)}, u32[]{:S(2)}, u32[]{:S(2)}) collective-permute-start(bf16[256,3840]{1,0:T(8,128)(2,1)} %pad_maximum_fusion.1.w0), channel_id=1, source_target_pairs={{0,2},{1,5},{2,0},{3,7},{4,6},{5,1},{6,4},{7,3},{8,10},{9,13},{10,... | collective-permute-start | bytes 5898248 | tf_op jit(solution)/shard_map/ppermute | solution.py:56
  148.8 37.3 %collective-permute-start.4 = (bf16[256,3072]{1,0:T(8,128)(2,1)}, bf16[256,3072]{1,0:T(8,128)(2,1)S(1)}, u32[]{:S(2)}, u32[]{:S(2)}) collective-permute-start(bf16[256,3072]{1,0:T(8,128)(2,1)} %pad_maximum_fusion.2.w0.s0), channel_id=1, source_target_pairs={{0,1},{1,0},{2,3},{3,2},{4,5},{5,4},{6,7},{7,6},{8,9},{9,8},{10,11... | collective-permute-start | bytes 4718600 | tf_op jit(solution)/shard_map/ppermute | solution.py:57
  171.6 24.0 %collective-permute-start.5 = (bf16[256,3072]{1,0:T(8,128)(2,1)}, bf16[256,3072]{1,0:T(8,128)(2,1)}, u32[]{:S(2)}, u32[]{:S(2)}) collective-permute-start(bf16[256,3072]{1,0:T(8,128)(2,1)} %collective-permute-done.3.w1.s1), channel_id=1, source_target_pairs={{0,1},{1,0},{2,3},{3,2},{4,5},{5,4},{6,7},{7,6},{8,9},{9,8},{10,11... | collective-permute-start | bytes 4718600 | tf_op jit(solution)/shard_map/ppermute | solution.py:57
  176.4 67.8 %collective-permute-start.19 = (bf16[256,4608]{1,0:T(8,128)(2,1)}, bf16[256,4608]{1,0:T(8,128)(2,1)}, u32[]{:S(2)}, u32[]{:S(2)}) collective-permute-start(bf16[256,4608]{1,0:T(8,128)(2,1)} %pad_maximum_fusion.w0), channel_id=1, source_target_pairs={{0,1},{1,0},{2,3},{3,2},{4,5},{5,4},{6,7},{7,6},{8,9},{9,8},{10,11... | collective-permute-start | bytes 7077896 | tf_op jit(solution)/shard_map/ppermute | solution.py:57
  176.5 67.8 %collective-permute-start.20 = (bf16[256,4608]{1,0:T(8,128)(2,1)}, bf16[256,4608]{1,0:T(8,128)(2,1)}, u32[]{:S(2)}, u32[]{:S(2)}) collective-permute-start(bf16[256,4608]{1,0:T(8,128)(2,1)} %collective-permute-done.18.w1), channel_id=1, source_target_pairs={{0,1},{1,0},{2,3},{3,2},{4,5},{5,4},{6,7},{7,6},{8,9},{9,8},{10,11... | collective-permute-start | bytes 7077896 | tf_op jit(solution)/shard_map/ppermute | solution.py:57
  186.1 73.7 %collective-permute-start.25 = (bf16[256,3840]{1,0:T(8,128)(2,1)}, bf16[256,3840]{1,0:T(8,128)(2,1)}, u32[]{:S(2)}, u32[]{:S(2)}) collective-permute-start(bf16[256,3840]{1,0:T(8,128)(2,1)} %pad_maximum_fusion.1.w0), channel_id=1, source_target_pairs={{0,1},{1,0},{2,3},{3,2},{4,5},{5,4},{6,7},{7,6},{8,9},{9,8},{10,11... | collective-permute-start | bytes 5898248 | tf_op jit(solution)/shard_map/ppermute | solution.py:57
  192.7 67.2 %collective-permute-start.26 = (bf16[256,3840]{1,0:T(8,128)(2,1)}, bf16[256,3840]{1,0:T(8,128)(2,1)}, u32[]{:S(2)}, u32[]{:S(2)}) collective-permute-start(bf16[256,3840]{1,0:T(8,128)(2,1)} %collective-permute-done.24.w1), channel_id=1, source_target_pairs={{0,1},{1,0},{2,3},{3,2},{4,5},{5,4},{6,7},{7,6},{8,9},{9,8},{10,11... | collective-permute-start | bytes 5898248 | tf_op jit(solution)/shard_map/ppermute | solution.py:57
  195.6 8.4 %collective-permute-start.12 = (bf16[1024,128]{1,0:T(8,128)(2,1)}, bf16[1024,128]{1,0:T(8,128)(2,1)S(1)}, u32[]{:S(2)}, u32[]{:S(2)}) collective-permute-start(bf16[1024,128]{1,0:T(8,128)(2,1)} %get-tuple-element.156), channel_id=1, source_target_pairs={{0,8},{1,9},{2,10},{3,11},{4,12},{5,13},{6,14},{7,15},{8,0},{9,1},... | collective-permute-start | bytes 786440 | tf_op jit(solution)/shard_map/ppermute | solution.py:82
  204.1 14.1 %collective-permute-start.13 = (bf16[1024,128]{1,0:T(8,128)(2,1)}, bf16[1024,128]{1,0:T(8,128)(2,1)S(1)}, u32[]{:S(2)}, u32[]{:S(2)}) collective-permute-start(bf16[1024,128]{1,0:T(8,128)(2,1)} %get-tuple-element.155), channel_id=1, source_target_pairs={{0,16},{1,17},{2,18},{3,19},{4,20},{5,21},{6,22},{7,23},{8,24},{9,... | collective-permute-start | bytes 786440 | tf_op jit(solution)/shard_map/ppermute | solution.py:82
  218.2 14.0 %collective-permute-start.14 = (bf16[1024,128]{1,0:T(8,128)(2,1)S(1)}, bf16[1024,128]{1,0:T(8,128)(2,1)S(1)}, u32[]{:S(2)}, u32[]{:S(2)}) collective-permute-start(bf16[1024,128]{1,0:T(8,128)(2,1)S(1)} %get-tuple-element.154), channel_id=1, source_target_pairs={{0,24},{1,25},{2,26},{3,27},{4,28},{5,29},{6,30},{7,31},{8,16},{9,... | collective-permute-start | bytes 786440 | tf_op jit(solution)/shard_map/ppermute | solution.py:82
  316.6 3.7 collective-permute-start.31
  319.1 93.5 %collective-permute-start.54 = (bf16[256,4608]{1,0:T(8,128)(2,1)}, bf16[256,4608]{1,0:T(8,128)(2,1)S(1)}, u32[]{:S(2)}, u32[]{:S(2)}) collective-permute-start(bf16[256,4608]{1,0:T(8,128)(2,1)} %get-tuple-element.117), channel_id=1, source_target_pairs={{0,1},{1,0},{2,3},{3,2},{4,5},{5,4},{6,7},{7,6},{8,9},{9,8},{10,11... | collective-permute-start | bytes 7077896 | tf_op jit(solution)/shard_map/ppermute | solution.py:62
  320.4 8.0 %collective-permute-start.32 = (f32[28,128]{1,0:T(8,128)S(1)}, f32[28,128]{1,0:T(8,128)S(1)}, u32[]{:S(2)}, u32[]{:S(2)}) collective-permute-start(f32[28,128]{1,0:T(8,128)S(1)} %add.202), channel_id=1, source_target_pairs={{0,4},{1,5},{2,6},{3,7},{4,0},{5,1},{6,2},{7,3},{8,12},{9,13},{10,... | collective-permute-start | bytes 43016 | tf_op jit(solution)/shard_map/ppermute | solution.py:75
  323.9 27.5 %collective-permute-start.27 = (bf16[1024,128]{1,0:T(8,128)(2,1)S(1)}, bf16[1024,128]{1,0:T(8,128)(2,1)S(1)}, u32[]{:S(2)}, u32[]{:S(2)}) collective-permute-start(bf16[1024,128]{1,0:T(8,128)(2,1)S(1)} %get-tuple-element.152), channel_id=1, source_target_pairs={{0,8},{1,9},{2,10},{3,11},{4,12},{5,13},{6,14},{7,15},{8,0},{9,1},... | collective-permute-start | bytes 786440 | tf_op jit(solution)/shard_map/ppermute | solution.py:82
  324.6 27.4 %collective-permute-start.28 = (bf16[1024,128]{1,0:T(8,128)(2,1)S(1)}, bf16[1024,128]{1,0:T(8,128)(2,1)S(1)}, u32[]{:S(2)}, u32[]{:S(2)}) collective-permute-start(bf16[1024,128]{1,0:T(8,128)(2,1)S(1)} %get-tuple-element.151), channel_id=1, source_target_pairs={{0,16},{1,17},{2,18},{3,19},{4,20},{5,21},{6,22},{7,23},{8,24},{9,... | collective-permute-start | bytes 786440 | tf_op jit(solution)/shard_map/ppermute | solution.py:82
  324.8 28.5 %collective-permute-start.29 = (bf16[1024,128]{1,0:T(8,128)(2,1)}, bf16[1024,128]{1,0:T(8,128)(2,1)}, u32[]{:S(2)}, u32[]{:S(2)}) collective-permute-start(bf16[1024,128]{1,0:T(8,128)(2,1)} %get-tuple-element.150), channel_id=1, source_target_pairs={{0,24},{1,25},{2,26},{3,27},{4,28},{5,29},{6,30},{7,31},{8,16},{9,... | collective-permute-start | bytes 786440 | tf_op jit(solution)/shard_map/ppermute | solution.py:82
  328.3 12.6 %collective-permute-start.33 = (f32[28,128]{1,0:T(8,128)S(1)}, f32[28,128]{1,0:T(8,128)S(1)}, u32[]{:S(2)}, u32[]{:S(2)}) collective-permute-start(f32[28,128]{1,0:T(8,128)S(1)} %add.203), channel_id=1, source_target_pairs={{0,8},{1,9},{2,10},{3,11},{4,12},{5,13},{6,14},{7,15},{8,0},{9,1},... | collective-permute-start | bytes 43016 | tf_op jit(solution)/shard_map/ppermute | solution.py:75
  341.0 9.1 %collective-permute-start.34 = (f32[28,128]{1,0:T(8,128)S(1)}, f32[28,128]{1,0:T(8,128)S(1)}, u32[]{:S(2)}, u32[]{:S(2)}) collective-permute-start(f32[28,128]{1,0:T(8,128)S(1)} %add.204), channel_id=1, source_target_pairs={{0,16},{1,17},{2,18},{3,19},{4,20},{5,21},{6,22},{7,23},{8,24},{9,... | collective-permute-start | bytes 43016 | tf_op jit(solution)/shard_map/ppermute | solution.py:75
  350.0 19.5 %collective-permute-start.48 = (bf16[256,2048]{1,0:T(8,128)(2,1)}, bf16[256,2048]{1,0:T(8,128)(2,1)}, u32[]{:S(2)}, u32[]{:S(2)}) collective-permute-start(bf16[256,2048]{1,0:T(8,128)(2,1)} %get-tuple-element.113), channel_id=1, source_target_pairs={{0,1},{1,0},{2,3},{3,2},{4,5},{5,4},{6,7},{7,6},{8,9},{9,8},{10,11... | collective-permute-start | bytes 3145736 | tf_op jit(solution)/shard_map/ppermute | solution.py:62
  351.4 24.6 %collective-permute-start.60 = (bf16[256,3840]{1,0:T(8,128)(2,1)}, bf16[256,3840]{1,0:T(8,128)(2,1)}, u32[]{:S(2)}, u32[]{:S(2)}) collective-permute-start(bf16[256,3840]{1,0:T(8,128)(2,1)} %get-tuple-element.121), channel_id=1, source_target_pairs={{0,1},{1,0},{2,3},{3,2},{4,5},{5,4},{6,7},{7,6},{8,9},{9,8},{10,11... | collective-permute-start | bytes 5898248 | tf_op jit(solution)/shard_map/ppermute | solution.py:62
  352.8 26.4 %collective-permute-start.47 = (bf16[256,2048]{1,0:T(8,128)(2,1)}, bf16[256,2048]{1,0:T(8,128)(2,1)S(1)}, u32[]{:S(2)}, u32[]{:S(2)}) collective-permute-start(bf16[256,2048]{1,0:T(8,128)(2,1)} %get-tuple-element.111), channel_id=1, source_target_pairs={{0,1},{1,0},{2,3},{3,2},{4,5},{5,4},{6,7},{7,6},{8,9},{9,8},{10,11... | collective-permute-start | bytes 3145736 | tf_op jit(solution)/shard_map/ppermute | solution.py:62
  353.3 18.6 %collective-permute-start.36 = (bf16[256,2048]{1,0:T(8,128)(2,1)}, bf16[256,2048]{1,0:T(8,128)(2,1)}, u32[]{:S(2)}, u32[]{:S(2)}) collective-permute-start(bf16[256,2048]{1,0:T(8,128)(2,1)} %get-tuple-element.103), channel_id=1, source_target_pairs={{0,1},{1,0},{2,3},{3,2},{4,5},{5,4},{6,7},{7,6},{8,9},{9,8},{10,11... | collective-permute-start | bytes 3145736 | tf_op jit(solution)/shard_map/ppermute | solution.py:62
  369.5 4.6 collective-permute-start.42
  371.9 18.9 %collective-permute-start.35 = (bf16[256,2048]{1,0:T(8,128)(2,1)S(1)}, bf16[256,2048]{1,0:T(8,128)(2,1)S(1)}, u32[]{:S(2)}, u32[]{:S(2)}) collective-permute-start(bf16[256,2048]{1,0:T(8,128)(2,1)S(1)} %copy-done.33), channel_id=1, source_target_pairs={{0,1},{1,0},{2,3},{3,2},{4,5},{5,4},{6,7},{7,6},{8,9},{9,8},{10,11... | collective-permute-start | bytes 3145736 | tf_op jit(solution)/shard_map/ppermute | solution.py:62
  374.1 14.9 %collective-permute-start.49 = (bf16[256,2048]{1,0:T(8,128)(2,1)S(1)}, bf16[256,2048]{1,0:T(8,128)(2,1)S(1)}, u32[]{:S(2)}, u32[]{:S(2)}) collective-permute-start(bf16[256,2048]{1,0:T(8,128)(2,1)S(1)} %add_convert_fusion.2), channel_id=1, source_target_pairs={{0,2},{1,5},{2,0},{3,7},{4,6},{5,1},{6,4},{7,3},{8,10},{9,13},{10,... | collective-permute-start | bytes 3145736 | tf_op jit(solution)/shard_map/ppermute | solution.py:65
  376.0 24.2 %collective-permute-start.37 = (bf16[256,2048]{1,0:T(8,128)(2,1)S(1)}, bf16[256,2048]{1,0:T(8,128)(2,1)S(1)}, u32[]{:S(2)}, u32[]{:S(2)}) collective-permute-start(bf16[256,2048]{1,0:T(8,128)(2,1)S(1)} %add_convert_fusion.4), channel_id=1, source_target_pairs={{0,2},{1,5},{2,0},{3,7},{4,6},{5,1},{6,4},{7,3},{8,10},{9,13},{10,... | collective-permute-start | bytes 3145736 | tf_op jit(solution)/shard_map/ppermute | solution.py:65
  379.2 21.7 %collective-permute-start.41 = (bf16[256,2048]{1,0:T(8,128)(2,1)S(1)}, bf16[256,2048]{1,0:T(8,128)(2,1)S(1)}, u32[]{:S(2)}, u32[]{:S(2)}) collective-permute-start(bf16[256,2048]{1,0:T(8,128)(2,1)S(1)} %copy-done.34), channel_id=1, source_target_pairs={{0,1},{1,0},{2,3},{3,2},{4,5},{5,4},{6,7},{7,6},{8,9},{9,8},{10,11... | collective-permute-start | bytes 3145736 | tf_op jit(solution)/shard_map/ppermute | solution.py:62
  389.0 22.5 %collective-permute-start.43 = (bf16[256,2048]{1,0:T(8,128)(2,1)S(1)}, bf16[256,2048]{1,0:T(8,128)(2,1)S(1)}, u32[]{:S(2)}, u32[]{:S(2)}) collective-permute-start(bf16[256,2048]{1,0:T(8,128)(2,1)S(1)} %add_convert_fusion.3), channel_id=1, source_target_pairs={{0,2},{1,5},{2,0},{3,7},{4,6},{5,1},{6,4},{7,3},{8,10},{9,13},{10,... | collective-permute-start | bytes 3145736 | tf_op jit(solution)/shard_map/ppermute | solution.py:65
  391.9 96.1 %collective-permute-start.53 = (bf16[256,4608]{1,0:T(8,128)(2,1)S(1)}, bf16[256,4608]{1,0:T(8,128)(2,1)S(1)}, u32[]{:S(2)}, u32[]{:S(2)}) collective-permute-start(bf16[256,4608]{1,0:T(8,128)(2,1)S(1)} %copy-done.31), channel_id=1, source_target_pairs={{0,1},{1,0},{2,3},{3,2},{4,5},{5,4},{6,7},{7,6},{8,9},{9,8},{10,11... | collective-permute-start | bytes 7077896 | tf_op jit(solution)/shard_map/ppermute | solution.py:62
  400.2 86.1 %collective-permute-start.59 = (bf16[256,3840]{1,0:T(8,128)(2,1)S(1)}, bf16[256,3840]{1,0:T(8,128)(2,1)S(1)}, u32[]{:S(2)}, u32[]{:S(2)}) collective-permute-start(bf16[256,3840]{1,0:T(8,128)(2,1)S(1)} %copy-done.32), channel_id=1, source_target_pairs={{0,1},{1,0},{2,3},{3,2},{4,5},{5,4},{6,7},{7,6},{8,9},{9,8},{10,11... | collective-permute-start | bytes 5898248 | tf_op jit(solution)/shard_map/ppermute | solution.py:62
  400.9 85.5 %collective-permute-start.61 = (bf16[256,3840]{1,0:T(8,128)(2,1)S(1)}, bf16[256,3840]{1,0:T(8,128)(2,1)S(1)}, u32[]{:S(2)}, u32[]{:S(2)}) collective-permute-start(bf16[256,3840]{1,0:T(8,128)(2,1)S(1)} %add_convert_fusion.1), channel_id=1, source_target_pairs={{0,2},{1,5},{2,0},{3,7},{4,6},{5,1},{6,4},{7,3},{8,10},{9,13},{10,... | collective-permute-start | bytes 5898248 | tf_op jit(solution)/shard_map/ppermute | solution.py:65
  411.5 14.9 %collective-permute-start.50 = (bf16[128,2048]{1,0:T(8,128)(2,1)S(1)}, bf16[128,2048]{1,0:T(8,128)(2,1)S(1)}, u32[]{:S(2)}, u32[]{:S(2)}) collective-permute-start(bf16[128,2048]{1,0:T(8,128)(2,1)S(1)} %slice.660), channel_id=1, source_target_pairs={{0,4},{1,3},{2,6},{3,1},{4,0},{5,7},{6,2},{7,5},{8,12},{9,11},{10,... | collective-permute-start | bytes 1572872 | tf_op jit(solution)/shard_map/ppermute | solution.py:68
  412.6 25.0 %collective-permute-start.38 = (bf16[128,2048]{1,0:T(8,128)(2,1)S(1)}, bf16[128,2048]{1,0:T(8,128)(2,1)S(1)}, u32[]{:S(2)}, u32[]{:S(2)}) collective-permute-start(bf16[128,2048]{1,0:T(8,128)(2,1)S(1)} %slice.662), channel_id=1, source_target_pairs={{0,4},{1,3},{2,6},{3,1},{4,0},{5,7},{6,2},{7,5},{8,12},{9,11},{10,... | collective-permute-start | bytes 1572872 | tf_op jit(solution)/shard_map/ppermute | solution.py:68
  426.3 22.5 %collective-permute-start.44 = (bf16[128,2048]{1,0:T(8,128)(2,1)S(1)}, bf16[128,2048]{1,0:T(8,128)(2,1)S(1)}, u32[]{:S(2)}, u32[]{:S(2)}) collective-permute-start(bf16[128,2048]{1,0:T(8,128)(2,1)S(1)} %slice.661), channel_id=1, source_target_pairs={{0,4},{1,3},{2,6},{3,1},{4,0},{5,7},{6,2},{7,5},{8,12},{9,11},{10,... | collective-permute-start | bytes 1572872 | tf_op jit(solution)/shard_map/ppermute | solution.py:68
  437.6 6.6 %collective-permute-start.51 = (bf16[64,2048]{1,0:T(8,128)(2,1)S(1)}, bf16[64,2048]{1,0:T(8,128)(2,1)S(1)}, u32[]{:S(2)}, u32[]{:S(2)}) collective-permute-start(bf16[64,2048]{1,0:T(8,128)(2,1)S(1)} %slice.665), channel_id=1, source_target_pairs={{0,8},{1,9},{2,10},{3,11},{4,12},{5,13},{6,14},{7,15},{8,0},{9,1},... | collective-permute-start | bytes 786440 | tf_op jit(solution)/shard_map/ppermute | solution.py:68
  444.2 43.8 %collective-permute-start.55 = (bf16[256,4608]{1,0:T(8,128)(2,1)S(1)}, bf16[256,4608]{1,0:T(8,128)(2,1)S(1)}, u32[]{:S(2)}, u32[]{:S(2)}) collective-permute-start(bf16[256,4608]{1,0:T(8,128)(2,1)S(1)} %add_convert_fusion), channel_id=1, source_target_pairs={{0,2},{1,5},{2,0},{3,7},{4,6},{5,1},{6,4},{7,3},{8,10},{9,13},{10,... | collective-permute-start | bytes 7077896 | tf_op jit(solution)/shard_map/ppermute | solution.py:65
  448.8 6.6 %collective-permute-start.39 = (bf16[64,2048]{1,0:T(8,128)(2,1)S(1)}, bf16[64,2048]{1,0:T(8,128)(2,1)S(1)}, u32[]{:S(2)}, u32[]{:S(2)}) collective-permute-start(bf16[64,2048]{1,0:T(8,128)(2,1)S(1)} %slice.667), channel_id=1, source_target_pairs={{0,8},{1,9},{2,10},{3,11},{4,12},{5,13},{6,14},{7,15},{8,0},{9,1},... | collective-permute-start | bytes 786440 | tf_op jit(solution)/shard_map/ppermute | solution.py:68
  455.4 9.6 %collective-permute-start.52 = (bf16[32,2048]{1,0:T(8,128)(2,1)S(1)}, bf16[32,2048]{1,0:T(8,128)(2,1)S(1)}, u32[]{:S(2)}, u32[]{:S(2)}) collective-permute-start(bf16[32,2048]{1,0:T(8,128)(2,1)S(1)} %slice.669), channel_id=1, source_target_pairs={{0,16},{1,17},{2,18},{3,19},{4,20},{5,21},{6,22},{7,23},{8,24},{9,... | collective-permute-start | bytes 393224 | tf_op jit(solution)/shard_map/ppermute | solution.py:68
  465.0 6.0 %collective-permute-start.40 = (bf16[32,2048]{1,0:T(8,128)(2,1)S(1)}, bf16[32,2048]{1,0:T(8,128)(2,1)S(1)}, u32[]{:S(2)}, u32[]{:S(2)}) collective-permute-start(bf16[32,2048]{1,0:T(8,128)(2,1)S(1)} %slice.671), channel_id=1, source_target_pairs={{0,16},{1,17},{2,18},{3,19},{4,20},{5,21},{6,22},{7,23},{8,24},{9,... | collective-permute-start | bytes 393224 | tf_op jit(solution)/shard_map/ppermute | solution.py:68
  471.0 7.8 %collective-permute-start.45 = (bf16[64,2048]{1,0:T(8,128)(2,1)S(1)}, bf16[64,2048]{1,0:T(8,128)(2,1)S(1)}, u32[]{:S(2)}, u32[]{:S(2)}) collective-permute-start(bf16[64,2048]{1,0:T(8,128)(2,1)S(1)} %slice.666), channel_id=1, source_target_pairs={{0,8},{1,9},{2,10},{3,11},{4,12},{5,13},{6,14},{7,15},{8,0},{9,1},... | collective-permute-start | bytes 786440 | tf_op jit(solution)/shard_map/ppermute | solution.py:68
  478.9 6.8 %collective-permute-start.46 = (bf16[32,2048]{1,0:T(8,128)(2,1)S(1)}, bf16[32,2048]{1,0:T(8,128)(2,1)S(1)}, u32[]{:S(2)}, u32[]{:S(2)}) collective-permute-start(bf16[32,2048]{1,0:T(8,128)(2,1)S(1)} %slice.670), channel_id=1, source_target_pairs={{0,16},{1,17},{2,18},{3,19},{4,20},{5,21},{6,22},{7,23},{8,24},{9,... | collective-permute-start | bytes 393224 | tf_op jit(solution)/shard_map/ppermute | solution.py:68
  487.3 14.2 %collective-permute-start.62 = (bf16[128,3840]{1,0:T(8,128)(2,1)S(1)}, bf16[128,3840]{1,0:T(8,128)(2,1)S(1)}, u32[]{:S(2)}, u32[]{:S(2)}) collective-permute-start(bf16[128,3840]{1,0:T(8,128)(2,1)S(1)} %slice.658), channel_id=1, source_target_pairs={{0,4},{1,3},{2,6},{3,1},{4,0},{5,7},{6,2},{7,5},{8,12},{9,11},{10,... | collective-permute-start | bytes 2949128 | tf_op jit(solution)/shard_map/ppermute | solution.py:68
  489.0 25.2 %collective-permute-start.56 = (bf16[128,4608]{1,0:T(8,128)(2,1)S(1)}, bf16[128,4608]{1,0:T(8,128)(2,1)S(1)}, u32[]{:S(2)}, u32[]{:S(2)}) collective-permute-start(bf16[128,4608]{1,0:T(8,128)(2,1)S(1)} %slice.657), channel_id=1, source_target_pairs={{0,4},{1,3},{2,6},{3,1},{4,0},{5,7},{6,2},{7,5},{8,12},{9,11},{10,... | collective-permute-start | bytes 3538952 | tf_op jit(solution)/shard_map/ppermute | solution.py:68
  501.7 13.2 %collective-permute-start.63 = (bf16[64,3840]{1,0:T(8,128)(2,1)S(1)}, bf16[64,3840]{1,0:T(8,128)(2,1)S(1)}, u32[]{:S(2)}, u32[]{:S(2)}) collective-permute-start(bf16[64,3840]{1,0:T(8,128)(2,1)S(1)} %slice.663), channel_id=1, source_target_pairs={{0,8},{1,9},{2,10},{3,11},{4,12},{5,13},{6,14},{7,15},{8,0},{9,1},... | collective-permute-start | bytes 1474568 | tf_op jit(solution)/shard_map/ppermute | solution.py:68
  514.4 14.2 %collective-permute-start.57 = (bf16[64,4608]{1,0:T(8,128)(2,1)S(1)}, bf16[64,4608]{1,0:T(8,128)(2,1)S(1)}, u32[]{:S(2)}, u32[]{:S(2)}) collective-permute-start(bf16[64,4608]{1,0:T(8,128)(2,1)S(1)} %slice.659), channel_id=1, source_target_pairs={{0,8},{1,9},{2,10},{3,11},{4,12},{5,13},{6,14},{7,15},{8,0},{9,1},... | collective-permute-start | bytes 1769480 | tf_op jit(solution)/shard_map/ppermute | solution.py:68
  515.0 13.8 %collective-permute-start.64 = (bf16[32,3840]{1,0:T(8,128)(2,1)S(1)}, bf16[32,3840]{1,0:T(8,128)(2,1)S(1)}, u32[]{:S(2)}, u32[]{:S(2)}) collective-permute-start(bf16[32,3840]{1,0:T(8,128)(2,1)S(1)} %slice.668), channel_id=1, source_target_pairs={{0,16},{1,17},{2,18},{3,19},{4,20},{5,21},{6,22},{7,23},{8,24},{9,... | collective-permute-start | bytes 737288 | tf_op jit(solution)/shard_map/ppermute | solution.py:68
  528.8 12.2 %collective-permute-start.58 = (bf16[32,4608]{1,0:T(8,128)(2,1)S(1)}, bf16[32,4608]{1,0:T(8,128)(2,1)S(1)}, u32[]{:S(2)}, u32[]{:S(2)}) collective-permute-start(bf16[32,4608]{1,0:T(8,128)(2,1)S(1)} %slice.664), channel_id=1, source_target_pairs={{0,16},{1,17},{2,18},{3,19},{4,20},{5,21},{6,22},{7,23},{8,24},{9,... | collective-permute-start | bytes 884744 | tf_op jit(solution)/shard_map/ppermute | solution.py:68
  (41 other events, 589.0 us)
